TPU v7x, 32 devices: a whole 2x2x4 slice. The times are simulated.
32 devices in a mesh: band: 4 (over y, x), tile: 8 (over z, core).
Axes of the slice: x: 2, y: 2, z: 4, core: 2. Of those that a mesh axis runs over, the one named last changes fastest.
Arguments:
- winds: float32 [2, 8, 48, 64, 720], P(None, None, 'band', 'tile'), may hold values from -8 to 8
- basis: bfloat16 [24, 48, 2, 64, 720], P(None, 'band', None, 'tile'), may hold values from -48 to 48
- ground: int32 [64, 720], P('tile'), may hold values from 24 to 48
Outputs:
- new_basis: float32 [24, 48, 2, 64, 720], P(None, 'band', None, 'tile')
All inputs are finite; a program needn't handle non-finite values.
Results may differ from a plain program's by a relative error of at most 0.0015.
Values sent between devices are 32-bit elements; how exact they have to be, the bound alone decides.
No kernel may reach another device: no remote copies, remote signals or barrier semaphores. Data moves between devices by JAX's collectives and lax.ppermute only.
A program may use at most 128 MiB of HBM per device.

v0:
```python
import jax
import jax.numpy as jnp
from jax import lax
from jax.experimental import pallas as pl
from jax.experimental.pallas import tpu as pltpu
from jax.sharding import PartitionSpec as P

ITERS = 4
HIGH = lax.Precision.HIGHEST
LON = 8
GROUP = 4
MIB = 1 << 20
F32 = jnp.float32
BF16 = jnp.bfloat16


def rows_of(shape):
    return lax.broadcasted_iota(jnp.int32, shape, len(shape) - 2)


def lanes_of(shape):
    return lax.broadcasted_iota(jnp.int32, shape, len(shape) - 1)


def gather_rows(planes, first):
    row = rows_of(planes[0].shape)
    out = None
    for i in reversed(range(GROUP)):
        shift = (2 * i - first) % LON
        moved = pltpu.roll(planes[i], shift, 0) if shift else planes[i]
        out = moved if out is None else jnp.where(row < 2 * (i + 1), moved, out)
    return out


def pack_kernel(winds, up, down):
    fields, _, levels = winds.shape[:3]
    for f in range(fields):
        for g in range(levels // GROUP):
            planes = [winds[f, 0, g * GROUP + i] for i in range(GROUP)]
            up[f, 0, g] = gather_rows(planes, LON - 2)
            down[f, 0, g] = gather_rows(planes, 0)


def pack(winds):
    fields, snaps, levels, lon, lat = winds.shape
    groups = levels // GROUP
    out = jax.ShapeDtypeStruct((fields, snaps, groups, lon, lat), F32)
    spec = pl.BlockSpec((fields, 1, groups, lon, lat), lambda t: (0, t, 0, 0, 0))
    return pl.pallas_call(
        pack_kernel,
        grid=(snaps,),
        in_specs=[pl.BlockSpec((fields, 1, levels, lon, lat), lambda t: (0, t, 0, 0, 0))],
        out_specs=[spec, spec],
        out_shape=[out, out],
        compiler_params=pltpu.CompilerParams(vmem_limit_bytes=32 * MIB),
        name="pack_halo",
    )(winds)


def lat_diff(x):
    lat = x.shape[1]
    wide = pl.cdiv(lat + 2, 128) * 128
    x = jnp.concatenate([x, jnp.zeros((LON, wide - lat), F32)], axis=1)
    near = pltpu.roll(x, wide - 1, 1) - pltpu.roll(x, 1, 1)
    far = pltpu.roll(x, wide - 2, 1) - pltpu.roll(x, 2, 1)
    return (8.0 * near - far)[:, :lat]


def lon_diff_inside(x):
    row = rows_of(x.shape)
    out = jnp.where(row < 7, 8.0 * pltpu.roll(x, 7, 0), 0.0)
    out = out - jnp.where(row > 0, 8.0 * pltpu.roll(x, 1, 0), 0.0)
    out = out - jnp.where(row < 6, pltpu.roll(x, 6, 0), 0.0)
    return out + jnp.where(row > 1, pltpu.roll(x, 2, 0), 0.0)


def same_lon(shape):
    return rows_of(shape) % LON == lanes_of(shape) % LON


def lon_trace(prod):
    rows, cols = prod.shape
    kept = jnp.where(same_lon(prod.shape), prod, 0.0)
    kept = jnp.sum(kept.reshape(rows // LON, LON, cols), axis=1)
    one = (rows_of((cols, cols // LON)) // LON == lanes_of((cols, cols // LON))).astype(F32)
    return jnp.dot(kept, one, precision=HIGH, preferred_element_type=F32)


def dot_lanes(a, b):
    return lax.dot_general(a, b, (((1,), (1,)), ((), ())), preferred_element_type=F32)


def local_kernel(winds, basis, ground, rows, partial, flat, gram, acc):
    level = pl.program_id(0)
    snaps, lat = winds.shape[1], winds.shape[4]
    rank = basis.shape[0]

    @pl.when(level == 0)
    def _():
        acc[...] = jnp.zeros_like(acc)

    cosine = jnp.broadcast_to(rows[0:1, :], (LON, lat))
    scale = jnp.where(level < ground[...], jnp.broadcast_to(rows[1:2, :], (LON, lat)), 0.0)
    for t in range(snaps):
        east, north = winds[0, t, 0], winds[1, t, 0]
        partial[0, 0, t] = (lon_diff_inside(north) - lat_diff(east * cosine)) * scale
        partial[0, 1, t] = (lon_diff_inside(east) + lat_diff(north * cosine)) * scale
    for f in range(2):
        block = basis[:, 0, f].astype(F32).reshape(rank * LON, lat).astype(BF16)
        flat[0, f] = block
        acc[...] += dot_lanes(block, block)

    @pl.when(level == pl.num_programs(0) - 1)
    def _():
        gram[...] = lon_trace(acc[...])


def local(winds, basis, ground, rows):
    fields, snaps, levels, lon, lat = winds.shape
    rank = basis.shape[0]
    return pl.pallas_call(
        local_kernel,
        grid=(levels,),
        in_specs=[
            pl.BlockSpec((fields, snaps, 1, lon, lat), lambda l: (0, 0, l, 0, 0)),
            pl.BlockSpec((rank, 1, fields, lon, lat), lambda l: (0, l, 0, 0, 0)),
            pl.BlockSpec((lon, lat), lambda l: (0, 0)),
            pl.BlockSpec((LON, lat), lambda l: (0, 0)),
        ],
        out_specs=[
            pl.BlockSpec((1, fields, snaps, lon, lat), lambda l: (l, 0, 0, 0, 0)),
            pl.BlockSpec((1, fields, rank * lon, lat), lambda l: (l, 0, 0, 0)),
            pl.BlockSpec((rank, rank), lambda l: (0, 0)),
        ],
        out_shape=[
            jax.ShapeDtypeStruct((levels, fields, snaps, lon, lat), F32),
            jax.ShapeDtypeStruct((levels, fields, rank * lon, lat), BF16),
            jax.ShapeDtypeStruct((rank, rank), F32),
        ],
        scratch_shapes=[pltpu.VMEM((rank * lon, rank * lon), F32)],
        compiler_params=pltpu.CompilerParams(vmem_limit_bytes=32 * MIB),
        cost_estimate=pl.CostEstimate(
            flops=2 * 10**9, bytes_accessed=26 * 10**6, transcendentals=0
        ),
        name="local_stencil",
    )(winds, basis, ground, rows)


def edge_kernel(partial, before, after, ground, rows, flat, gram_basis, snap, gram, acc_b, acc_s):
    level = pl.program_id(0)
    snaps, lat = partial.shape[2], partial.shape[4]
    rank = gram_basis.shape[0]

    @pl.when(level == 0)
    def _():
        acc_b[...] = jnp.zeros_like(acc_b)
        acc_s[...] = jnp.zeros_like(acc_s)

    scale = jnp.where(level < ground[...], jnp.broadcast_to(rows[1:2, :], (LON, lat)), 0.0)
    row = rows_of((LON, lat))
    place = 2 * lax.rem(level, GROUP)
    low = jnp.where(row == 0, -8.0 * scale, scale)
    high = jnp.where(row == 7, 8.0 * scale, -scale)
    for f in range(2):
        planes = []
        for t in range(snaps):
            b = pltpu.roll(before[1 - f, t, 0], LON - place, 0)
            a = pltpu.roll(after[1 - f, t, 0], LON - 2 - place, 0)
            near_b = jnp.where(row == 0, pltpu.roll(b, 7, 0), b)
            near_a = jnp.where(row == 7, pltpu.roll(a, 1, 0), a)
            edge = jnp.where(row < 2, near_b * low, jnp.where(row > 5, near_a * high, 0.0))
            far = jnp.where(row == 0, b * scale, jnp.where(row == 7, -a * scale, 0.0))
            planes.append(partial[0, f, t] + (edge + far))
        block = jnp.concatenate(planes, axis=0).astype(BF16)
        snap[0, f] = block
        acc_b[...] += dot_lanes(block, flat[0, f])
        acc_s[...] += dot_lanes(block, block)

    @pl.when(level == pl.num_programs(0) - 1)
    def _():
        cross = lon_trace(acc_b[...])
        gram[0:rank, 0:rank] = gram_basis[...]
        gram[rank:, 0:rank] = cross
        gram[rank:, rank:] = lon_trace(acc_s[...])
        gram[0:rank, rank:] = cross.T


def edges(partial, before, after, ground, rows, flat, gram_basis):
    levels, fields, snaps, lon, lat = partial.shape
    rank = gram_basis.shape[0]
    cols = rank + snaps
    halo = pl.BlockSpec((fields, snaps, 1, lon, lat), lambda l: (0, 0, l // GROUP, 0, 0))
    return pl.pallas_call(
        edge_kernel,
        grid=(levels,),
        in_specs=[
            pl.BlockSpec((1, fields, snaps, lon, lat), lambda l: (l, 0, 0, 0, 0)),
            halo,
            halo,
            pl.BlockSpec((lon, lat), lambda l: (0, 0)),
            pl.BlockSpec((LON, lat), lambda l: (0, 0)),
            pl.BlockSpec((1, fields, rank * lon, lat), lambda l: (l, 0, 0, 0)),
            pl.BlockSpec((rank, rank), lambda l: (0, 0)),
        ],
        out_specs=[
            pl.BlockSpec((1, fields, snaps * lon, lat), lambda l: (l, 0, 0, 0)),
            pl.BlockSpec((cols, cols), lambda l: (0, 0)),
        ],
        out_shape=[
            jax.ShapeDtypeStruct((levels, fields, snaps * lon, lat), BF16),
            jax.ShapeDtypeStruct((cols, cols), F32),
        ],
        scratch_shapes=[
            pltpu.VMEM((snaps * lon, rank * lon), F32),
            pltpu.VMEM((snaps * lon, snaps * lon), F32),
        ],
        compiler_params=pltpu.CompilerParams(vmem_limit_bytes=32 * MIB),
        name="edge_gram",
    )(partial, before, after, ground, rows, flat, gram_basis)


def sweep(block, rank):
    lane = lanes_of(block.shape)
    for j in range(rank):
        column = jnp.broadcast_to(block[:, j : j + 1], block.shape)
        norm = jnp.sum(column * column, axis=0, keepdims=True)
        along = jnp.sum(column * block, axis=0, keepdims=True)
        part = jnp.where(lane[:1] > j, along / norm, 0.0)
        block = block - column * part
    norm = jnp.sum(block * block, axis=0, keepdims=True)
    return jnp.where(lane < rank, block / jnp.sqrt(norm), 0.0)


def frame_of(gram, rank):
    cols = gram.shape[0]
    lane, row = lanes_of(gram.shape), rows_of(gram.shape)
    frame = sweep(gram, rank)
    for _ in range(ITERS - 1):
        frame = sweep(jnp.dot(gram, frame, precision=HIGH, preferred_element_type=F32), rank)
    dots = lax.dot_general(
        frame, frame, (((0,), (0,)), ((), ())), precision=HIGH, preferred_element_type=F32
    )
    upper = jnp.where(row < lane, dots, 0.0)
    upper = upper + jnp.where(row == lane, 0.5 * (dots - 1.0), 0.0)
    upper = jnp.where(lane < rank, upper, 0.0)
    return frame - jnp.dot(frame, upper, precision=HIGH, preferred_element_type=F32)


def final_kernel(grams, flat, snap, out, lhs, held, sems):
    level = pl.program_id(0)
    rank = out.shape[0]
    wide = flat.shape[2]
    copies = [
        pltpu.make_async_copy(flat, held.at[:, :, 0:wide], sems.at[0]),
        pltpu.make_async_copy(snap, held.at[:, :, wide:], sems.at[1]),
    ]

    @pl.when(level == 0)
    def _():
        for copy in copies:
            copy.start()
        frame = frame_of(jnp.sum(grams[...], axis=0), rank)
        cols = frame.shape[0]
        high = frame.astype(BF16).astype(F32)
        low = frame - high
        spread = (rows_of((cols, cols * LON)) == lanes_of((cols, cols * LON)) // LON).astype(BF16)
        for i, part in enumerate((high, low)):
            wide_t = lax.dot_general(
                part.astype(BF16), spread, (((0,), (0,)), ((), ())), preferred_element_type=F32
            )[:rank]
            tall = jnp.broadcast_to(wide_t[:, None, :], (rank, LON, cols * LON))
            tall = tall.reshape(rank * LON, cols * LON)
            tall = jnp.where(same_lon(tall.shape), tall, 0.0)
            lhs[i * rank * LON : (i + 1) * rank * LON, :] = tall.astype(BF16)
        for copy in copies:
            copy.wait()

    for f in range(2):
        both = jnp.dot(lhs[...], held[level, f], preferred_element_type=F32)
        total = both[: rank * LON] + both[rank * LON :]
        out[:, 0, f] = total.reshape(rank, LON, total.shape[1])


def final(grams, flat, snap, rank):
    levels, fields, _, lat = flat.shape
    cols = grams.shape[-1]
    return pl.pallas_call(
        final_kernel,
        grid=(levels,),
        in_specs=[
            pl.BlockSpec(grams.shape, lambda l: (0, 0, 0)),
            pl.BlockSpec(memory_space=pl.ANY),
            pl.BlockSpec(memory_space=pl.ANY),
        ],
        out_specs=pl.BlockSpec((rank, 1, fields, LON, lat), lambda l: (0, l, 0, 0, 0)),
        out_shape=jax.ShapeDtypeStruct((rank, levels, fields, LON, lat), F32),
        scratch_shapes=[
            pltpu.VMEM((2 * rank * LON, cols * LON), BF16),
            pltpu.VMEM((levels, fields, cols * LON, lat), BF16),
            pltpu.SemaphoreType.DMA((2,)),
        ],
        compiler_params=pltpu.CompilerParams(vmem_limit_bytes=40 * MIB),
        name="frame_project",
    )(grams, flat, snap)


def on_device(winds, basis, ground):
    levels, lat = winds.shape[2], winds.shape[4]
    rank = basis.shape[0]
    tiles = lax.axis_size("tile")
    devices = tiles * lax.axis_size("band")
    up_pairs = [(i, (i + 1) % tiles) for i in range(tiles)]
    down_pairs = [(j, i) for i, j in up_pairs]

    up, down = pack(winds)
    before = lax.ppermute(up, "tile", up_pairs)
    after = lax.ppermute(down, "tile", down_pairs)

    cosine = jnp.cos((jnp.arange(lat, dtype=F32) + 0.5) * (jnp.pi / lat) - jnp.pi / 2)
    rows = jnp.stack([cosine, jnp.sqrt(cosine) / cosine / 12.0])
    rows = jnp.concatenate([rows, jnp.zeros((LON - 2, lat), F32)])
    ground = ground - lax.axis_index("band") * levels
    partial, flat, gram_basis = local(winds, basis, ground, rows)
    snap, gram = edges(partial, before, after, ground, rows, flat, gram_basis)
    copies = jnp.broadcast_to(gram[None], (devices,) + gram.shape)
    grams = lax.all_to_all(copies, ("band", "tile"), 0, 0)
    return final(grams, flat, snap, rank)


def solution(mesh):
    return jax.shard_map(
        on_device,
        mesh=mesh,
        in_specs=(
            P(None, None, "band", "tile", None),
            P(None, "band", None, "tile", None),
            P("tile", None),
        ),
        out_specs=P(None, "band", None, "tile", None),
        check_vma=False,
    )
```

profile of v0, /device:TPU:0, one launch (start us, length us, event | category | flops | bytes accessed | tf_op | source)
XLA Modules:
  0.0 82.9 jit_solution(13293909953209857081)
XLA Ops:
  0.0 2.3 %copy-done.2 = f32[2,8,12,8,720]{4,3,2,1,0:T(8,128)S(1)} copy-done((f32[2,8,12,8,720]{4,3,2,1,0:T(8,128)S(1)}, f32[2,8,12,8,720]{4,3,2,1,0:T(8,128)}, u32[]{:S(2)}) %copy-start.2) | copy-done | bytes 4423704
  2.3 3.2 %pack_halo.1 = (f32[2,8,3,8,720]{4,3,2,1,0:T(8,128)}, f32[2,8,3,8,720]{4,3,2,1,0:T(8,128)S(1)}) custom-call(f32[2,8,12,8,720]{4,3,2,1,0:T(8,128)S(1)} %copy-done.2), custom_call_target="tpu_custom_call" | custom-call | tf_op jit(solution)/shard_map/pack_halo/pallas_call | solution.py:49
  5.6 0.5 collective-permute-start
  6.0 4.0 %collective-permute-start.1 = (f32[2,8,3,8,720]{4,3,2,1,0:T(8,128)S(1)}, f32[2,8,3,8,720]{4,3,2,1,0:T(8,128)S(1)}, u32[]{:S(2)}, u32[]{:S(2)}) collective-permute-start(f32[2,8,3,8,720]{4,3,2,1,0:T(8,128)S(1)} %get-tuple-element.14), channel_id=1, source_target_pairs={{1,0},{2,1},{3,2},{4,3},{5,4},{6,5},{7,6},{0,7},{9,8},{10,9},{11,1... | collective-permute-start | bytes 3317768 | tf_op jit(solution)/shard_map/ppermute | solution.py:317
  10.0 0.1 pad.2.clone
  10.1 0.1 fusion
  10.2 0.1 maximum_maximum_fusion.rows
  10.3 0.7 broadcast_subtract_fusion.ground
  11.1 2.3 %copy-done.3 = f32[2,8,12,8,720]{4,3,2,1,0:T(8,128)S(1)} copy-done((f32[2,8,12,8,720]{4,3,2,1,0:T(8,128)S(1)}, f32[2,8,12,8,720]{4,3,2,1,0:T(8,128)}, u32[]{:S(2)}) %copy-start.3) | copy-done | bytes 4423704
  13.4 10.8 %local_stencil.1 = (f32[12,2,8,8,720]{4,3,2,1,0:T(8,128)S(1)}, bf16[12,2,192,720]{3,2,1,0:T(8,128)(2,1)S(1)}, f32[24,24]{1,0:T(8,128)S(1)}) custom-call(f32[2,8,12,8,720]{4,3,2,1,0:T(8,128)S(1)} %copy-done.3, bf16[24,12,2,8,720]{4,3,2,1,0:T(8,128)(2,1)} %basis.1, s32[8,720]{1,0:T(8,128)S(1)} %broadcast_subtract_fusion.ground, ...), custom_call_target="tpu_custom_call" | custom-call | flops 2000000000 | bytes 26000000 | tf_op jit(solution)/shard_map/local_stencil/pallas_call | solution.py:121
  24.3 10.1 %collective-permute-done.before = f32[2,8,3,8,720]{4,3,2,1,0:T(8,128)S(1)} collective-permute-done((f32[2,8,3,8,720]{4,3,2,1,0:T(8,128)}, f32[2,8,3,8,720]{4,3,2,1,0:T(8,128)S(1)}, u32[]{:S(2)}, u32[]{:S(2)}) %collective-permute-start) | collective-permute-done | bytes 1105952 | tf_op jit(solution)/shard_map/ppermute | solution.py:316
  34.3 0.3 collective-permute-done.1.after
  34.6 1.0 %copy-done.4 = f32[2,8,3,8,720]{4,3,2,1,0:T(8,128)} copy-done((f32[2,8,3,8,720]{4,3,2,1,0:T(8,128)}, f32[2,8,3,8,720]{4,3,2,1,0:T(8,128)S(1)}, u32[]{:S(2)}) %copy-start.4) | copy-done | bytes 1105944
  35.6 1.3 %copy-done.5 = f32[2,8,3,8,720]{4,3,2,1,0:T(8,128)S(1)} copy-done((f32[2,8,3,8,720]{4,3,2,1,0:T(8,128)S(1)}, f32[2,8,3,8,720]{4,3,2,1,0:T(8,128)}, u32[]{:S(2)}) %copy-start.5) | copy-done | bytes 1105944
  36.9 6.3 %edge_gram.1 = (bf16[12,2,64,720]{3,2,1,0:T(8,128)(2,1)S(1)}, f32[32,32]{1,0:T(8,128)S(1)}) custom-call(f32[12,2,8,8,720]{4,3,2,1,0:T(8,128)S(1)} %get-tuple-element.12.partial, f32[2,8,3,8,720]{4,3,2,1,0:T(8,128)S(1)} %collective-permute-done.before, f32[2,8,3,8,720]{4,3,2,1,0:T(8,128)S(1)} %copy-done.5, s32[8,720]{1,0:T(8,128)S(1)} %broadcast_subtract_fusion.ground, ...), custom_call_target="tpu_custom_call" | custom-call | tf_op jit(solution)/shard_map/edge_gram/pallas_call | solution.py:193
  43.2 0.1 broadcast_in_dim.10
  43.3 0.3 reshape.27
  43.6 14.7 %all_to_all.5 = f32[32,1,1024]{2,1,0:T(1,128)S(1)} all-to-all(f32[32,1,1024]{2,1,0:T(1,128)S(1)} %reshape.27), channel_id=1, replica_groups=mesh['band'=4,'tile'=8] {'band','tile'}, dimensions={0} | all-to-all | bytes 262144 | tf_op jit(solution)/shard_map/all_to_all | solution.py:326
  58.3 0.6 broadcast.51
  58.8 0.9 %reduce = f32[32,1024]{1,0:T(8,128)S(1)} reduce(f32[32,1,1024]{2,1,0:T(1,128)S(1)} %all_to_all.5, f32[]{:T(128)} %broadcast.51), dimensions={1}, to_apply=%all_to_all.3.reduce_sub_computation | reduce | bytes 262148 | tf_op jit(solution)/shard_map/all_to_all | solution.py:326
  59.8 0.2 reshape.28.grams
  59.9 0.0 copy-start.1
  59.9 3.0 %copy-done.1 = bf16[12,2,192,720]{3,2,1,0:T(8,128)(2,1)S(1)} copy-done((bf16[12,2,192,720]{3,2,1,0:T(8,128)(2,1)S(1)}, bf16[12,2,192,720]{3,2,1,0:T(8,128)(2,1)}, u32[]{:S(2)}) %copy-start.1) | copy-done | bytes 6635544
  63.0 19.9 %frame_project.1 = f32[24,12,2,8,720]{4,3,2,1,0:T(8,128)} custom-call(f32[32,32,32]{2,1,0:T(8,128)S(1)} %reshape.28.grams, bf16[12,2,192,720]{3,2,1,0:T(8,128)(2,1)S(1)} %copy-done.1, bf16[12,2,64,720]{3,2,1,0:T(8,128)(2,1)S(1)} %get-tuple-element.18.snap), custom_call_target="tpu_custom_call" | custom-call | tf_op jit(solution)/shard_map/frame_project/pallas_call | solution.py:287
  (7 shorter events, 0.0 us)
Async XLA Ops:
  0.0 2.3 %copy-start.2 = (f32[2,8,12,8,720]{4,3,2,1,0:T(8,128)S(1)}, f32[2,8,12,8,720]{4,3,2,1,0:T(8,128)}, u32[]{:S(2)}) copy-start(f32[2,8,12,8,720]{4,3,2,1,0:T(8,128)} %winds.3) | copy-start | bytes 13271044
  5.6 28.8 %collective-permute-start = (f32[2,8,3,8,720]{4,3,2,1,0:T(8,128)}, f32[2,8,3,8,720]{4,3,2,1,0:T(8,128)S(1)}, u32[]{:S(2)}, u32[]{:S(2)}) collective-permute-start(f32[2,8,3,8,720]{4,3,2,1,0:T(8,128)} %get-tuple-element.13), channel_id=1, source_target_pairs={{0,1},{1,2},{2,3},{3,4},{4,5},{5,6},{6,7},{7,0},{8,9},{9,10},{10,1... | collective-permute-start | bytes 3317768 | tf_op jit(solution)/shard_map/ppermute | solution.py:316
  6.0 28.6 %collective-permute-start.1 = (f32[2,8,3,8,720]{4,3,2,1,0:T(8,128)S(1)}, f32[2,8,3,8,720]{4,3,2,1,0:T(8,128)S(1)}, u32[]{:S(2)}, u32[]{:S(2)}) collective-permute-start(f32[2,8,3,8,720]{4,3,2,1,0:T(8,128)S(1)} %get-tuple-element.14), channel_id=1, source_target_pairs={{1,0},{2,1},{3,2},{4,3},{5,4},{6,5},{7,6},{0,7},{9,8},{10,9},{11,1... | collective-permute-start | bytes 3317768 | tf_op jit(solution)/shard_map/ppermute | solution.py:317
  11.1 2.3 %copy-start.3 = (f32[2,8,12,8,720]{4,3,2,1,0:T(8,128)S(1)}, f32[2,8,12,8,720]{4,3,2,1,0:T(8,128)}, u32[]{:S(2)}) copy-start(f32[2,8,12,8,720]{4,3,2,1,0:T(8,128)} %winds.3) | copy-start | bytes 13271044
  24.2 18.9 %copy-start = (bf16[12,2,192,720]{3,2,1,0:T(8,128)(2,1)}, bf16[12,2,192,720]{3,2,1,0:T(8,128)(2,1)S(1)}, u32[]{:S(2)}) copy-start(bf16[12,2,192,720]{3,2,1,0:T(8,128)(2,1)S(1)} %get-tuple-element.15.flat) | copy-start | bytes 19906564
  34.6 1.0 %copy-start.4 = (f32[2,8,3,8,720]{4,3,2,1,0:T(8,128)}, f32[2,8,3,8,720]{4,3,2,1,0:T(8,128)S(1)}, u32[]{:S(2)}) copy-start(f32[2,8,3,8,720]{4,3,2,1,0:T(8,128)S(1)} %collective-permute-done.1.after) | copy-start | bytes 3317764
  35.6 1.3 %copy-start.5 = (f32[2,8,3,8,720]{4,3,2,1,0:T(8,128)S(1)}, f32[2,8,3,8,720]{4,3,2,1,0:T(8,128)}, u32[]{:S(2)}) copy-start(f32[2,8,3,8,720]{4,3,2,1,0:T(8,128)} %copy-done.4) | copy-start | bytes 3317764
  59.9 3.0 %copy-start.1 = (bf16[12,2,192,720]{3,2,1,0:T(8,128)(2,1)S(1)}, bf16[12,2,192,720]{3,2,1,0:T(8,128)(2,1)}, u32[]{:S(2)}) copy-start(bf16[12,2,192,720]{3,2,1,0:T(8,128)(2,1)} %copy-done) | copy-start | bytes 19906564
where the time goes:
time: 83.4 us; the launch traced here: 82.9 us
  Pallas kernels  40.2 us (48%)
  blocking collectives  14.7 us (18%)
  local copies, waits for them, and re-layouts  11.2 us (13%)
  waiting for transfers between devices  10.4 us (12%)
  starting transfers between devices  4.49 us (5%)
  other arithmetic  1.86 us (2%)
    pallas_call x1, Pallas kernels, final(): pl.pallas_call(final_kernel, grid=(levels,), in_specs=[pl.BlockSpec(grams...  19.9 us
    all_to_all x1, blocking collectives, on_device(): grams = lax.all_to_all(copies, ('band', 'tile'), 0, 0)  14.7 us
    pallas_call x1, Pallas kernels, local(): pl.pallas_call(local_kernel, grid=(levels,), in_specs=[pl.BlockSpec((fiel...  10.8 us
    unnamed x14, local copies, waits for them, and re-layouts  10.4 us
    ppermute x1, waiting for transfers between devices, on_device(): before = lax.ppermute(up, 'tile', up_pairs)  10.1 us
    pallas_call x1, Pallas kernels, edges(): pl.pallas_call(edge_kernel, grid=(levels,), in_specs=[pl.BlockSpec((1, fi...  6.27 us
    ppermute x1, starting transfers between devices, on_device(): after = lax.ppermute(down, 'tile', down_pairs)  4.04 us
    pallas_call x1, Pallas kernels, pack(): pl.pallas_call(pack_kernel, grid=(snaps,), in_specs=[pl.BlockSpec((fields...  3.21 us
  transfers between devices with their start and end apart: 2, of which 2 were waited for; matrix products, arithmetic and copies ran while one was open for 1% of the time, Pallas kernels for 13%

commit v1 on v0

v1 whole, which is shorter than its diff:
```python
import jax
import jax.numpy as jnp
from jax import lax
from jax.experimental import pallas as pl
from jax.experimental.pallas import tpu as pltpu
from jax.sharding import PartitionSpec as P

ITERS = 4
HIGH = lax.Precision.HIGHEST
LON = 8
HALF = 4
TURN = 3
MIB = 1 << 20
F32 = jnp.float32
BF16 = jnp.bfloat16


def rows_of(shape):
    return lax.broadcasted_iota(jnp.int32, shape, len(shape) - 2)


def lanes_of(shape):
    return lax.broadcasted_iota(jnp.int32, shape, len(shape) - 1)


def turn_of(levels):
    return TURN if levels % TURN == 0 else 1


def whole_lanes(lat):
    return lat // 128 * 128


def ordered(row, at2, at4, at6, rest):
    return jnp.where(row < 2, at2, jnp.where(row < 4, at4, jnp.where(row < 6, at6, rest)))


def pack_kernel(winds, up, down):
    fields, snaps, turn = winds.shape[:3]
    lat = winds.shape[4]
    main = whole_lanes(lat)
    row = rows_of((LON, lat))
    odd = row % 2 == 1
    for f in range(fields):
        for g in range(snaps // 4):
            tails = ([], [])
            for i in range(turn):
                x = [winds[f, 4 * g + t, i] for t in range(4)]
                both2, both6 = pltpu.roll(x[2], 2, 0), pltpu.roll(x[3], 6, 0)
                low = ordered(row, x[0], both2, pltpu.roll(x[1], 4, 0), both6)
                low = jnp.where(odd, 8.0 * pltpu.roll(low, 1, 0), 0.0) - low
                high = ordered(row, both2, pltpu.roll(x[0], 4, 0), both6, x[1])
                high = high - jnp.where(odd, 0.0, 8.0 * pltpu.roll(high, 7, 0))
                for ref, tail, tile in ((down, tails[0], low), (up, tails[1], high)):
                    ref[f, 0, g, :, i * main : (i + 1) * main] = tile[:, :main]
                    tail.append(tile[:, main:])
            for ref, tail in ((down, tails[0]), (up, tails[1])):
                ref[f, 0, g, :, turn * main :] = jnp.concatenate(tail, axis=1)


def pack(winds):
    fields, snaps, levels, lon, lat = winds.shape
    turn = turn_of(levels)
    out = jax.ShapeDtypeStruct((fields, levels // turn, snaps // 4, lon, turn * lat), F32)
    spec = pl.BlockSpec((fields, 1) + out.shape[2:], lambda i: (0, i, 0, 0, 0))
    return pl.pallas_call(
        pack_kernel,
        grid=(levels // turn,),
        in_specs=[pl.BlockSpec((fields, snaps, turn, lon, lat), lambda i: (0, 0, i, 0, 0))],
        out_specs=[spec, spec],
        out_shape=[out, out],
        compiler_params=pltpu.CompilerParams(vmem_limit_bytes=60 * MIB),
        name="pack_halo",
    )(winds)


def lat_diff(x):
    lat = x.shape[1]
    wide = pl.cdiv(lat + 2, 128) * 128
    x = jnp.concatenate([x, jnp.zeros((LON, wide - lat), F32)], axis=1)
    near = pltpu.roll(x, wide - 1, 1) - pltpu.roll(x, 1, 1)
    far = pltpu.roll(x, wide - 2, 1) - pltpu.roll(x, 2, 1)
    return (8.0 * near - far)[:, :lat]


def lon_diff_inside(x):
    row = rows_of(x.shape)
    out = jnp.where(row < 7, 8.0 * pltpu.roll(x, 7, 0), 0.0)
    out = out - jnp.where(row > 0, 8.0 * pltpu.roll(x, 1, 0), 0.0)
    out = out - jnp.where(row < 6, pltpu.roll(x, 6, 0), 0.0)
    return out + jnp.where(row > 1, pltpu.roll(x, 2, 0), 0.0)


def parted(planes):
    inner, edge = [], []
    for one, two in zip(planes[::2], planes[1::2]):
        top = rows_of(one.shape) < HALF
        one2, one6 = pltpu.roll(one, 2, 0), pltpu.roll(one, 6, 0)
        two2, two6 = pltpu.roll(two, 2, 0), pltpu.roll(two, 6, 0)
        inner.append(jnp.where(top, one6, two2))
        edge.append(jnp.where(top, one2, two6))
    return jnp.concatenate(inner, axis=0), jnp.concatenate(edge, axis=0)


def lon_trace(prod):
    rows, cols = prod.shape
    kept = jnp.where(rows_of(prod.shape) % HALF == lanes_of(prod.shape) % HALF, prod, 0.0)
    left = (lanes_of((rows // HALF, rows)) // HALF == rows_of((rows // HALF, rows))).astype(F32)
    right = (rows_of((cols, cols // HALF)) // HALF == lanes_of((cols, cols // HALF))).astype(F32)
    kept = jnp.dot(left, kept, precision=HIGH, preferred_element_type=F32)
    return jnp.dot(kept, right, precision=HIGH, preferred_element_type=F32)


def dot_lanes(a, b):
    return lax.dot_general(a, b, (((1,), (1,)), ((), ())), preferred_element_type=F32)


def local_kernel(
    winds, basis, ground, rows, edge, basis_edge, inner, basis_inner, gram, acc_inner, acc_edge
):
    level = pl.program_id(0)
    snaps, lat = winds.shape[1], winds.shape[4]
    rank = basis.shape[0]

    @pl.when(level == 0)
    def _():
        acc_inner[...] = jnp.zeros_like(acc_inner)
        acc_edge[...] = jnp.zeros_like(acc_edge)

    cosine = jnp.broadcast_to(rows[0:1, :], (LON, lat))
    scale = jnp.where(level < ground[...], jnp.broadcast_to(rows[1:2, :], (LON, lat)), 0.0)
    fields = ([], [])
    for t in range(snaps):
        east, north = winds[0, t, 0], winds[1, t, 0]
        fields[0].append((lon_diff_inside(north) - lat_diff(east * cosine)) * scale)
        fields[1].append((lon_diff_inside(east) + lat_diff(north * cosine)) * scale)
    for f in range(2):
        inside, outside = parted(fields[f])
        edge[0, f] = outside
        inside = inside.astype(BF16)
        inner[0, f] = inside
        b_inside, b_outside = parted([basis[c, 0, f].astype(F32) for c in range(rank)])
        b_inside, b_outside = b_inside.astype(BF16), b_outside.astype(BF16)
        basis_inner[0, f] = b_inside
        basis_edge[0, f] = b_outside
        block = jnp.concatenate([b_inside, inside], axis=0)
        acc_inner[...] += dot_lanes(block, block)
        acc_edge[...] += dot_lanes(b_outside, b_outside)

    @pl.when(level == pl.num_programs(0) - 1)
    def _():
        gram[...] = lon_trace(acc_inner[...])
        gram[0:rank, 0:rank] += lon_trace(acc_edge[...])


def local(winds, basis, ground, rows):
    fields, snaps, levels, lon, lat = winds.shape
    rank = basis.shape[0]
    cols = rank + snaps

    def each(height, dtype):
        block = pl.BlockSpec((1, fields, height, lat), lambda l: (l, 0, 0, 0))
        return block, jax.ShapeDtypeStruct((levels, fields, height, lat), dtype)

    outs = [
        each(snaps * HALF, F32),
        each(rank * HALF, BF16),
        each(snaps * HALF, BF16),
        each(rank * HALF, BF16),
        (
            pl.BlockSpec((cols, cols), lambda l: (0, 0)),
            jax.ShapeDtypeStruct((cols, cols), F32),
        ),
    ]
    return pl.pallas_call(
        local_kernel,
        grid=(levels,),
        in_specs=[
            pl.BlockSpec((fields, snaps, 1, lon, lat), lambda l: (0, 0, l, 0, 0)),
            pl.BlockSpec((rank, 1, fields, lon, lat), lambda l: (0, l, 0, 0, 0)),
            pl.BlockSpec((lon, lat), lambda l: (0, 0)),
            pl.BlockSpec((LON, lat), lambda l: (0, 0)),
        ],
        out_specs=[block for block, _ in outs],
        out_shape=[shape for _, shape in outs],
        scratch_shapes=[
            pltpu.VMEM((cols * HALF, cols * HALF), F32),
            pltpu.VMEM((rank * HALF, rank * HALF), F32),
        ],
        compiler_params=pltpu.CompilerParams(vmem_limit_bytes=40 * MIB),
        cost_estimate=pl.CostEstimate(
            flops=2 * 10**9, bytes_accessed=26 * 10**6, transcendentals=0
        ),
        name="local_stencil",
    )(winds, basis, ground, rows)


def edge_kernel(before, after, part, basis_edge, ground, rows, gram, snap, copies, held, acc, sems):
    levels, fields, height, lat = part.shape
    turns, groups = before.shape[1:3]
    turn = levels // turns
    main = whole_lanes(lat)
    rank = gram.shape[0] - height // HALF
    pulls = []
    for n in range(turns):
        for i, source in enumerate((before, after)):
            pulls.append(pltpu.make_async_copy(source.at[:, n], held.at[i, n], sems.at[i, n]))
            pulls[-1].start()
    acc[...] = jnp.zeros_like(acc)
    row = rows_of((LON, lat))
    from_after = row % HALF < 2

    def tile(side, n, f, g, i):
        start = turn * main + i * (lat - main)
        return jnp.concatenate(
            [
                held[side, n, f, g, :, i * main : (i + 1) * main],
                held[side, n, f, g, :, start : start + lat - main],
            ],
            axis=1,
        )

    for n in range(turns):
        pulls[2 * n].wait()
        pulls[2 * n + 1].wait()
        for i in range(turn):
            level = n * turn + i
            scale = jnp.where(level < ground[...], jnp.broadcast_to(rows[1:2, :], (LON, lat)), 0.0)
            for f in range(fields):
                tiles = []
                for g in range(groups):
                    high, low = tile(0, n, 1 - f, g, i), tile(1, n, 1 - f, g, i)
                    tiles.append(jnp.where(from_after, low, high))
                    tiles.append(
                        jnp.where(from_after, pltpu.roll(low, 6, 0), pltpu.roll(high, 2, 0))
                    )
                tiles = [
                    part[level, f, LON * p : LON * (p + 1)] + x * scale
                    for p, x in enumerate(tiles)
                ]
                block = jnp.concatenate(tiles, axis=0).astype(BF16)
                snap[level, f] = block
                both = jnp.concatenate([basis_edge[level, f], block], axis=0)
                acc[...] += dot_lanes(block, both)

    late = lon_trace(acc[...])
    cross = jnp.concatenate([jnp.zeros((rank, rank), F32), late[:, :rank].T], axis=1)
    total = gram[...] + jnp.concatenate([cross, late], axis=0)
    cols = total.shape[0]
    lined = jnp.concatenate([total[LON * p : LON * (p + 1)] for p in range(cols // LON)], axis=1)
    copies[...] = jnp.broadcast_to(lined[None], copies.shape)


def edges(before, after, part, basis_edge, ground, rows, gram, devices):
    levels, fields, height, lat = part.shape
    cols = gram.shape[0]
    whole = pl.BlockSpec(memory_space=pltpu.VMEM)
    far = pl.BlockSpec(memory_space=pl.ANY)
    turns, groups = before.shape[1:3]
    return pl.pallas_call(
        edge_kernel,
        in_specs=[far, far, whole, whole, whole, whole, whole],
        out_specs=[whole, whole],
        out_shape=[
            jax.ShapeDtypeStruct((levels, fields, height, lat), BF16),
            jax.ShapeDtypeStruct((devices, LON, cols * cols // LON), F32),
        ],
        scratch_shapes=[
            pltpu.VMEM((2, turns, fields, groups, LON, before.shape[4]), F32),
            pltpu.VMEM((height, cols * HALF), F32),
            pltpu.SemaphoreType.DMA((2, turns)),
        ],
        compiler_params=pltpu.CompilerParams(vmem_limit_bytes=40 * MIB),
        name="edge_gram",
    )(before, after, part, basis_edge, ground, rows, gram)


def spread_lane(block, j):
    return jnp.broadcast_to(block[:, j : j + 1], block.shape)


def down_sum(x):
    return jnp.sum(x, axis=0, keepdims=True)


def sweep(block, rank):
    lane = lanes_of(block.shape)
    ahead = [spread_lane(block, j) for j in range(2)]
    for j in range(rank):
        if j + 2 < rank:
            ahead.append(spread_lane(block, j + 2))
        column = ahead.pop(0)
        inverse = 1.0 / down_sum(column * column)
        ahead = [x - column * (down_sum(column * x) * inverse) for x in ahead]
        part = jnp.where(lane[:1] > j, down_sum(column * block) * inverse, 0.0)
        block = block - column * part
    norm = down_sum(block * block)
    return jnp.where(lane < rank, block / jnp.sqrt(norm), 0.0)


def frame_of(gram, rank):
    lane, row = lanes_of(gram.shape), rows_of(gram.shape)
    frame = sweep(gram, rank)
    for _ in range(ITERS - 1):
        frame = sweep(jnp.dot(gram, frame, precision=HIGH, preferred_element_type=F32), rank)
    dots = lax.dot_general(
        frame, frame, (((0,), (0,)), ((), ())), precision=HIGH, preferred_element_type=F32
    )
    upper = jnp.where(row < lane, dots, 0.0)
    upper = upper + jnp.where(row == lane, 0.5 * (dots - 1.0), 0.0)
    upper = jnp.where(lane < rank, upper, 0.0)
    return frame - jnp.dot(frame, upper, precision=HIGH, preferred_element_type=F32)


def frame_rows(frame, rank):
    cols = frame.shape[0]
    wide = cols * LON
    near = rank * HALF

    def column(index):
        late = index >= 2 * near
        base = jnp.where(late, index - 2 * near, index)
        size = jnp.where(late, wide // 2 - near, near)
        second = base >= size
        base = jnp.where(second, base - size, base)
        lon = jnp.where(second, (index % HALF + 6) % LON, index % HALF + 2)
        return base // HALF + jnp.where(late, rank, 0), lon

    which, _ = column(lanes_of((cols, wide)))
    spread = (rows_of((cols, wide)) == which).astype(BF16)
    shape = (rank * LON, wide)
    _, lon = column(lanes_of(shape))
    kept = rows_of(shape) % LON == lon
    high = frame.astype(BF16)
    low = (frame - high.astype(F32)).astype(BF16)
    parts = []
    for part in (high, low):
        flat = lax.dot_general(
            part, spread, (((0,), (0,)), ((), ())), preferred_element_type=F32
        )[:rank]
        tall = jnp.broadcast_to(flat[:, None, :], (rank, LON, wide)).reshape(shape)
        parts.append(jnp.where(kept, tall, 0.0).astype(BF16))
    return jnp.concatenate(parts, axis=0)


def final_kernel(grams, basis_inner, basis_edge, inner, edge, out, lhs, held, sems):
    level = pl.program_id(0)
    rank = out.shape[0]
    copies, at = [], 0
    for i, source in enumerate((basis_inner, basis_edge, inner, edge)):
        height = source.shape[2]
        copies.append(pltpu.make_async_copy(source, held.at[:, :, at : at + height], sems.at[i]))
        at += height

    @pl.when(level == 0)
    def _():
        for copy in copies:
            copy.start()
        lined = jnp.sum(grams[...], axis=0)
        cols = lined.shape[1] * LON // (held.shape[2] // LON)
        gram = jnp.concatenate(
            [lined[:, cols * p : cols * (p + 1)] for p in range(cols // LON)], axis=0
        )
        lhs[...] = frame_rows(frame_of(gram, rank), rank)
        for copy in copies:
            copy.wait()

    for f in range(2):
        both = jnp.dot(lhs[...], held[level, f], preferred_element_type=F32)
        total = both[: rank * LON] + both[rank * LON :]
        out[:, 0, f] = total.reshape(rank, LON, total.shape[1])


def final(grams, basis_inner, basis_edge, inner, edge):
    levels, fields, height, lat = basis_inner.shape
    rank = height // HALF
    cols = rank + inner.shape[2] // HALF
    far = pl.BlockSpec(memory_space=pl.ANY)
    return pl.pallas_call(
        final_kernel,
        grid=(levels,),
        in_specs=[pl.BlockSpec(grams.shape, lambda l: (0, 0, 0)), far, far, far, far],
        out_specs=pl.BlockSpec((rank, 1, fields, LON, lat), lambda l: (0, l, 0, 0, 0)),
        out_shape=jax.ShapeDtypeStruct((rank, levels, fields, LON, lat), F32),
        scratch_shapes=[
            pltpu.VMEM((2 * rank * LON, cols * LON), BF16),
            pltpu.VMEM((levels, fields, cols * LON, lat), BF16),
            pltpu.SemaphoreType.DMA((4,)),
        ],
        compiler_params=pltpu.CompilerParams(vmem_limit_bytes=40 * MIB),
        name="frame_project",
    )(grams, basis_inner, basis_edge, inner, edge)


def on_device(winds, basis, ground):
    levels, lat = winds.shape[2], winds.shape[4]
    tiles = lax.axis_size("tile")
    devices = tiles * lax.axis_size("band")
    up_pairs = [(i, (i + 1) % tiles) for i in range(tiles)]
    down_pairs = [(j, i) for i, j in up_pairs]

    up, down = pack(winds)
    before = lax.ppermute(up, "tile", up_pairs)
    after = lax.ppermute(down, "tile", down_pairs)

    cosine = jnp.cos((jnp.arange(lat, dtype=F32) + 0.5) * (jnp.pi / lat) - jnp.pi / 2)
    rows = jnp.stack([cosine, jnp.sqrt(cosine) / cosine / 12.0])
    rows = jnp.concatenate([rows, jnp.zeros((LON - 2, lat), F32)])
    ground = ground - lax.axis_index("band") * levels
    ground_edge = jnp.concatenate([ground[6:], ground[:2], ground[6:], ground[:2]])
    part, basis_edge, inner, basis_inner, gram = local(winds, basis, ground, rows)
    edge, copies = edges(before, after, part, basis_edge, ground_edge, rows, gram, devices)
    grams = lax.all_to_all(copies, ("band", "tile"), 0, 0)
    return final(grams, basis_inner, basis_edge, inner, edge)


def solution(mesh):
    return jax.shard_map(
        on_device,
        mesh=mesh,
        in_specs=(
            P(None, None, "band", "tile", None),
            P(None, "band", None, "tile", None),
            P("tile", None),
        ),
        out_specs=P(None, "band", None, "tile", None),
        check_vma=False,
    )
```

time: 83.4 us -> 66.1 us (0.79)
  local copies, waits for them, and re-layouts: 11.2 us -> 0.09 us
  Pallas kernels: 40.2 us -> 37.4 us
  other arithmetic: 1.86 us -> 0.21 us
  waiting for transfers between devices: 10.4 us -> 8.87 us
    unnamed x14 -> x2, local copies, waits for them, and re-layouts: 10.4 us -> 0.01 us
    pallas_call x1, Pallas kernels: 19.9 us -> 15.2 us  [final(): pl.pallas_call(final_kernel, grid=(levels,), in_specs=[pl.BlockSpec(grams...]
    pallas_call x1, Pallas kernels: 10.8 us -> 14.1 us  [local(): pl.pallas_call(local_kernel, grid=(levels,), in_specs=[pl.BlockSpec((fiel...]
    ppermute x1, waiting for transfers between devices: 10.1 us -> 8.25 us  [on_device(): before = lax.ppermute(up, 'tile', up_pairs)]
    pallas_call x2, Pallas kernels: 9.48 us -> 8.12 us  [the longest x1 4.63 us: pack(): pl.pallas_call(pack_kernel, grid=(levels // turn,), in_specs=[pl.BlockSpe...]
    all_to_all x1 -> x0, other arithmetic: 0.93 us -> none  [on_device(): grams = lax.all_to_all(copies, ('band', 'tile'), 0, 0)]
  transfers between devices with their start and end apart: 2 -> 2, of which waited for: 2 -> 2; matrix products, arithmetic and copies ran while one was open for 1% -> 0% of each run, Pallas kernels for 13% -> 21%
where the time goes in v1:
time: 66.1 us; the launch traced here: 65.7 us
  Pallas kernels  37.4 us (57%)
  blocking collectives  14.6 us (22%)
  waiting for transfers between devices  8.87 us (13%)
  starting transfers between devices  4.49 us (7%)
    pallas_call x1, Pallas kernels, final(): pl.pallas_call(final_kernel, grid=(levels,), in_specs=[pl.BlockSpec(grams...  15.2 us
    all_to_all x1, blocking collectives, on_device(): grams = lax.all_to_all(copies, ('band', 'tile'), 0, 0)  14.6 us
    pallas_call x1, Pallas kernels, local(): pl.pallas_call(local_kernel, grid=(levels,), in_specs=[pl.BlockSpec((fiel...  14.1 us
    ppermute x1, waiting for transfers between devices, on_device(): before = lax.ppermute(up, 'tile', up_pairs)  8.25 us
    pallas_call x1, Pallas kernels, pack(): pl.pallas_call(pack_kernel, grid=(levels // turn,), in_specs=[pl.BlockSpe...  4.63 us
    ppermute x1, starting transfers between devices, on_device(): after = lax.ppermute(down, 'tile', down_pairs)  4.04 us
    pallas_call x1, Pallas kernels, edges(): pl.pallas_call(edge_kernel, in_specs=[far, far, whole, whole, whole, whol...  3.49 us
  transfers between devices with their start and end apart: 2, of which 2 were waited for; matrix products, arithmetic and copies ran while one was open for 0% of the time, Pallas kernels for 21%

profile of v1, /device:TPU:0, one launch (start us, length us, event | category | flops | bytes accessed | tf_op | source)
XLA Modules:
  0.0 65.7 jit_solution(2306700515409841562)
XLA Ops:
  0.0 0.0 copy-start
  0.0 4.6 %pack_halo.1 = (f32[2,4,2,8,2160]{4,3,2,1,0:T(8,128)}, f32[2,4,2,8,2160]{4,3,2,1,0:T(8,128)}) custom-call(f32[2,8,12,8,720]{4,3,2,1,0:T(8,128)} %winds.3), custom_call_target="tpu_custom_call" | custom-call | tf_op jit(solution)/shard_map/pack_halo/pallas_call | solution.py:66
  4.6 0.5 collective-permute-start
  5.1 4.0 %collective-permute-start.1 = (f32[2,4,2,8,2160]{4,3,2,1,0:T(8,128)}, f32[2,4,2,8,2160]{4,3,2,1,0:T(8,128)S(1)}, u32[]{:S(2)}, u32[]{:S(2)}) collective-permute-start(f32[2,4,2,8,2160]{4,3,2,1,0:T(8,128)} %get-tuple-element.15), channel_id=1, source_target_pairs={{1,0},{2,1},{3,2},{4,3},{5,4},{6,5},{7,6},{0,7},{9,8},{10,9},{11,1... | collective-permute-start | bytes 3317768 | tf_op jit(solution)/shard_map/ppermute | solution.py:404
  9.1 0.1 pad.6.clone
  9.2 0.1 fusion
  9.3 0.0 copy-done
  9.4 0.1 maximum_maximum_fusion.rows
  9.5 14.1 %local_stencil.1 = (f32[12,2,32,720]{3,2,1,0:T(8,128)S(1)}, bf16[12,2,96,720]{3,2,1,0:T(8,128)(2,1)S(1)}, bf16[12,2,32,720]{3,2,1,0:T(8,128)(2,1)S(1)}, bf16[12,2,96,720]{3,2,1,0:T(8,128)(2,1)S(1)}, f32[32,32]{1,0:T(8,128)S(1)}) custom-call(f32[2,8,12,8,720]{4,3,2,1,0:T(8,128)} %winds.3, bf16[24,12,2,8,720]{4,3,2,1,0:T(8,128)(2,1)} %basis.1, ...), custom_call_target="tpu_custom_call" | custom-call | flops 2000000000 | bytes 26000000 | tf_op jit(solution)/shard_map/local_stencil/pallas_call | solution.py:175
  23.5 8.3 %collective-permute-done.before = f32[2,4,2,8,2160]{4,3,2,1,0:T(8,128)S(1)} collective-permute-done((f32[2,4,2,8,2160]{4,3,2,1,0:T(8,128)}, f32[2,4,2,8,2160]{4,3,2,1,0:T(8,128)S(1)}, u32[]{:S(2)}, u32[]{:S(2)}) %collective-permute-start) | collective-permute-done | bytes 1105952 | tf_op jit(solution)/shard_map/ppermute | solution.py:403
  31.8 0.6 collective-permute-done.1.after
  32.4 3.5 %edge_gram.1 = (bf16[12,2,32,720]{3,2,1,0:T(8,128)(2,1)S(1)}, f32[32,8,128]{2,1,0:T(8,128)S(1)}) custom-call(f32[2,4,2,8,2160]{4,3,2,1,0:T(8,128)S(1)} %collective-permute-done.before, f32[2,4,2,8,2160]{4,3,2,1,0:T(8,128)S(1)} %collective-permute-done.1.after, f32[12,2,32,720]{3,2,1,0:T(8,128)S(1)} %get-tuple-element.16.part, ...), custom_call_target="tpu_custom_call" | custom-call | tf_op jit(solution)/shard_map/edge_gram/pallas_call | solution.py:260
  35.9 14.6 %all_to_all.5.grams = f32[32,8,128]{2,1,0:T(8,128)S(1)} all-to-all(f32[32,8,128]{2,1,0:T(8,128)S(1)} %get-tuple-element.19), channel_id=1, replica_groups=mesh['band'=4,'tile'=8] {'band','tile'}, dimensions={0} | all-to-all | bytes 262144 | tf_op jit(solution)/shard_map/all_to_all | solution.py:413
  50.5 15.2 %frame_project.1 = f32[24,12,2,8,720]{4,3,2,1,0:T(8,128)} custom-call(f32[32,8,128]{2,1,0:T(8,128)S(1)} %all_to_all.5.grams, bf16[12,2,96,720]{3,2,1,0:T(8,128)(2,1)S(1)} %get-tuple-element.20.basis_inner, bf16[12,2,96,720]{3,2,1,0:T(8,128)(2,1)S(1)} %get-tuple-element.17.basis_edge, bf16[12,2,32,720]{3,2,1,0:T(8,128)(2,1)S(1)} %get-tuple-element.21.inner, ...), custom_call_target="tpu_custom_call" | custom-call | tf_op jit(solution)/shard_map/frame_project/pallas_call | solution.py:379
  (4 shorter events, 0.0 us)
Async XLA Ops:
  0.0 9.3 %copy-start = (s32[8,720]{1,0:T(8,128)S(1)}, s32[8,720]{1,0:T(8,128)}, u32[]{:S(2)}) copy-start(s32[8,720]{1,0:T(8,128)} %param.5) | copy-start | bytes 69124
  4.6 27.2 %collective-permute-start = (f32[2,4,2,8,2160]{4,3,2,1,0:T(8,128)}, f32[2,4,2,8,2160]{4,3,2,1,0:T(8,128)S(1)}, u32[]{:S(2)}, u32[]{:S(2)}) collective-permute-start(f32[2,4,2,8,2160]{4,3,2,1,0:T(8,128)} %get-tuple-element.14), channel_id=1, source_target_pairs={{0,1},{1,2},{2,3},{3,4},{4,5},{5,6},{6,7},{7,0},{8,9},{9,10},{10,1... | collective-permute-start | bytes 3317768 | tf_op jit(solution)/shard_map/ppermute | solution.py:403
  5.1 27.3 %collective-permute-start.1 = (f32[2,4,2,8,2160]{4,3,2,1,0:T(8,128)}, f32[2,4,2,8,2160]{4,3,2,1,0:T(8,128)S(1)}, u32[]{:S(2)}, u32[]{:S(2)}) collective-permute-start(f32[2,4,2,8,2160]{4,3,2,1,0:T(8,128)} %get-tuple-element.15), channel_id=1, source_target_pairs={{1,0},{2,1},{3,2},{4,3},{5,4},{6,5},{7,6},{0,7},{9,8},{10,9},{11,1... | collective-permute-start | bytes 3317768 | tf_op jit(solution)/shard_map/ppermute | solution.py:404

commit v2 on v1

--- a/solution.py
+++ b/solution.py
@@ -1,3 +1,5 @@
+import functools
+
 import jax
 import jax.numpy as jnp
 from jax import lax
@@ -11,6 +13,8 @@
 HALF = 4
 TURN = 3
 MIB = 1 << 20
+PACK_VMEM = 56 * MIB
+AHEAD = 4
 F32 = jnp.float32
 BF16 = jnp.bfloat16
 
@@ -27,6 +31,12 @@
     return TURN if levels % TURN == 0 else 1
 
 
+def spans_of(levels):
+    if levels % 2:
+        return [(0, levels)]
+    return [(0, levels // 2), (levels // 2, levels // 2)]
+
+
 def whole_lanes(lat):
     return lat // 128 * 128
 
@@ -35,43 +45,56 @@
     return jnp.where(row < 2, at2, jnp.where(row < 4, at4, jnp.where(row < 6, at6, rest)))
 
 
-def pack_kernel(winds, up, down):
-    fields, snaps, turn = winds.shape[:3]
+def pack_kernel(first, winds, *refs):
+    up, down, held, sems = refs[-4:]
+    fields, snaps = winds.shape[:2]
+    turns, turn = held.shape[0], held.shape[3]
     lat = winds.shape[4]
     main = whole_lanes(lat)
+    pulls = []
+    for n in range(turns):
+        levels = pl.ds(first + n * turn, turn)
+        pulls.append(pltpu.make_async_copy(winds.at[:, :, levels], held.at[n], sems.at[n]))
+        pulls[-1].start()
     row = rows_of((LON, lat))
     odd = row % 2 == 1
-    for f in range(fields):
-        for g in range(snaps // 4):
-            tails = ([], [])
-            for i in range(turn):
-                x = [winds[f, 4 * g + t, i] for t in range(4)]
-                both2, both6 = pltpu.roll(x[2], 2, 0), pltpu.roll(x[3], 6, 0)
-                low = ordered(row, x[0], both2, pltpu.roll(x[1], 4, 0), both6)
-                low = jnp.where(odd, 8.0 * pltpu.roll(low, 1, 0), 0.0) - low
-                high = ordered(row, both2, pltpu.roll(x[0], 4, 0), both6, x[1])
-                high = high - jnp.where(odd, 0.0, 8.0 * pltpu.roll(high, 7, 0))
-                for ref, tail, tile in ((down, tails[0], low), (up, tails[1], high)):
-                    ref[f, 0, g, :, i * main : (i + 1) * main] = tile[:, :main]
-                    tail.append(tile[:, main:])
-            for ref, tail in ((down, tails[0]), (up, tails[1])):
-                ref[f, 0, g, :, turn * main :] = jnp.concatenate(tail, axis=1)
-
-
-def pack(winds):
-    fields, snaps, levels, lon, lat = winds.shape
-    turn = turn_of(levels)
-    out = jax.ShapeDtypeStruct((fields, levels // turn, snaps // 4, lon, turn * lat), F32)
-    spec = pl.BlockSpec((fields, 1) + out.shape[2:], lambda i: (0, i, 0, 0, 0))
+    for n in range(turns):
+        pulls[n].wait()
+        for f in range(fields):
+            for g in range(snaps // 4):
+                tails = ([], [])
+                for i in range(turn):
+                    x = [held[n, f, 4 * g + t, i] for t in range(4)]
+                    both2, both6 = pltpu.roll(x[2], 2, 0), pltpu.roll(x[3], 6, 0)
+                    low = ordered(row, x[0], both2, pltpu.roll(x[1], 4, 0), both6)
+                    low = jnp.where(odd, 8.0 * pltpu.roll(low, 1, 0), 0.0) - low
+                    high = ordered(row, both2, pltpu.roll(x[0], 4, 0), both6, x[1])
+                    high = high - jnp.where(odd, 0.0, 8.0 * pltpu.roll(high, 7, 0))
+                    for ref, tail, tile in ((down, tails[0], low), (up, tails[1], high)):
+                        ref[f, n, g, :, i * main : (i + 1) * main] = tile[:, :main]
+                        tail.append(tile[:, main:])
+                for ref, tail in ((down, tails[0]), (up, tails[1])):
+                    ref[f, n, g, :, turn * main :] = jnp.concatenate(tail, axis=1)
+
+
+def pack(winds, first, count, after):
+    fields, snaps, _, lon, lat = winds.shape
+    turn = turn_of(count)
+    turns = count // turn
+    out = jax.ShapeDtypeStruct((fields, turns, snaps // 4, lon, turn * lat), F32)
+    whole = pl.BlockSpec(memory_space=pltpu.VMEM)
     return pl.pallas_call(
-        pack_kernel,
-        grid=(levels // turn,),
-        in_specs=[pl.BlockSpec((fields, snaps, turn, lon, lat), lambda i: (0, 0, i, 0, 0))],
-        out_specs=[spec, spec],
+        functools.partial(pack_kernel, first),
+        in_specs=[pl.BlockSpec(memory_space=pl.ANY)] * (1 + len(after)),
+        out_specs=[whole, whole],
         out_shape=[out, out],
-        compiler_params=pltpu.CompilerParams(vmem_limit_bytes=60 * MIB),
+        scratch_shapes=[
+            pltpu.VMEM((turns, fields, snaps, turn, lon, lat), F32),
+            pltpu.SemaphoreType.DMA((turns,)),
+        ],
+        compiler_params=pltpu.CompilerParams(vmem_limit_bytes=PACK_VMEM),
         name="pack_halo",
-    )(winds)
+    )(winds, *after)
 
 
 def lat_diff(x):
@@ -195,10 +218,12 @@
     )(winds, basis, ground, rows)
 
 
-def edge_kernel(before, after, part, basis_edge, ground, rows, gram, snap, copies, held, acc, sems):
-    levels, fields, height, lat = part.shape
+def edge_kernel(
+    first, last, before, after, part, basis_edge, ground, rows, gram, snap, out, held, acc, sems
+):
+    fields, height, lat = part.shape[1:]
     turns, groups = before.shape[1:3]
-    turn = levels // turns
+    turn = snap.shape[0] // turns
     main = whole_lanes(lat)
     rank = gram.shape[0] - height // HALF
     pulls = []
@@ -224,7 +249,8 @@
         pulls[2 * n].wait()
         pulls[2 * n + 1].wait()
         for i in range(turn):
-            level = n * turn + i
+            here = n * turn + i
+            level = first + here
             scale = jnp.where(level < ground[...], jnp.broadcast_to(rows[1:2, :], (LON, lat)), 0.0)
             for f in range(fields):
                 tiles = []
@@ -239,38 +265,46 @@
                     for p, x in enumerate(tiles)
                 ]
                 block = jnp.concatenate(tiles, axis=0).astype(BF16)
-                snap[level, f] = block
+                snap[here, f] = block
                 both = jnp.concatenate([basis_edge[level, f], block], axis=0)
                 acc[...] += dot_lanes(block, both)
 
     late = lon_trace(acc[...])
     cross = jnp.concatenate([jnp.zeros((rank, rank), F32), late[:, :rank].T], axis=1)
     total = gram[...] + jnp.concatenate([cross, late], axis=0)
+    if not last:
+        out[...] = total
+        return
     cols = total.shape[0]
     lined = jnp.concatenate([total[LON * p : LON * (p + 1)] for p in range(cols // LON)], axis=1)
-    copies[...] = jnp.broadcast_to(lined[None], copies.shape)
-
-
-def edges(before, after, part, basis_edge, ground, rows, gram, devices):
+    out[...] = jnp.broadcast_to(lined[None], out.shape)
+
+
+def edges(before, after, part, basis_edge, ground, rows, gram, first, count, devices):
     levels, fields, height, lat = part.shape
     cols = gram.shape[0]
+    last = first + count == levels
     whole = pl.BlockSpec(memory_space=pltpu.VMEM)
     far = pl.BlockSpec(memory_space=pl.ANY)
     turns, groups = before.shape[1:3]
+    shape = (devices, LON, cols * cols // LON) if last else (cols, cols)
     return pl.pallas_call(
-        edge_kernel,
+        functools.partial(edge_kernel, first, last),
         in_specs=[far, far, whole, whole, whole, whole, whole],
         out_specs=[whole, whole],
         out_shape=[
-            jax.ShapeDtypeStruct((levels, fields, height, lat), BF16),
-            jax.ShapeDtypeStruct((devices, LON, cols * cols // LON), F32),
+            jax.ShapeDtypeStruct((count, fields, height, lat), BF16),
+            jax.ShapeDtypeStruct(shape, F32),
         ],
         scratch_shapes=[
             pltpu.VMEM((2, turns, fields, groups, LON, before.shape[4]), F32),
             pltpu.VMEM((height, cols * HALF), F32),
             pltpu.SemaphoreType.DMA((2, turns)),
         ],
-        compiler_params=pltpu.CompilerParams(vmem_limit_bytes=40 * MIB),
+        compiler_params=pltpu.CompilerParams(vmem_limit_bytes=32 * MIB),
+        cost_estimate=pl.CostEstimate(
+            flops=10**8, bytes_accessed=6 * 10**6, transcendentals=0
+        ),
         name="edge_gram",
     )(before, after, part, basis_edge, ground, rows, gram)
 
@@ -285,10 +319,10 @@
 
 def sweep(block, rank):
     lane = lanes_of(block.shape)
-    ahead = [spread_lane(block, j) for j in range(2)]
+    ahead = [spread_lane(block, j) for j in range(AHEAD)]
     for j in range(rank):
-        if j + 2 < rank:
-            ahead.append(spread_lane(block, j + 2))
+        if j + AHEAD < rank:
+            ahead.append(spread_lane(block, j + AHEAD))
         column = ahead.pop(0)
         inverse = 1.0 / down_sum(column * column)
         ahead = [x - column * (down_sum(column * x) * inverse) for x in ahead]
@@ -343,53 +377,77 @@
     return jnp.concatenate(parts, axis=0)
 
 
-def final_kernel(grams, basis_inner, basis_edge, inner, edge, out, lhs, held, sems):
-    level = pl.program_id(0)
-    rank = out.shape[0]
-    copies, at = [], 0
-    for i, source in enumerate((basis_inner, basis_edge, inner, edge)):
+def final_kernel(grams, basis_inner, basis_edge, inner, *refs):
+    edge_parts, (out, lhs, held, made, in_sems, out_sems) = refs[:-6], refs[-6:]
+    rank, levels = out.shape[:2]
+    pulls, at = [], 0
+    for source in (basis_inner, basis_edge, inner):
         height = source.shape[2]
-        copies.append(pltpu.make_async_copy(source, held.at[:, :, at : at + height], sems.at[i]))
+        pulls.append((source, held.at[:, :, at : at + height]))
         at += height
-
-    @pl.when(level == 0)
-    def _():
-        for copy in copies:
-            copy.start()
-        lined = jnp.sum(grams[...], axis=0)
-        cols = lined.shape[1] * LON // (held.shape[2] // LON)
-        gram = jnp.concatenate(
-            [lined[:, cols * p : cols * (p + 1)] for p in range(cols // LON)], axis=0
-        )
-        lhs[...] = frame_rows(frame_of(gram, rank), rank)
-        for copy in copies:
-            copy.wait()
-
-    for f in range(2):
-        both = jnp.dot(lhs[...], held[level, f], preferred_element_type=F32)
-        total = both[: rank * LON] + both[rank * LON :]
-        out[:, 0, f] = total.reshape(rank, LON, total.shape[1])
-
-
-def final(grams, basis_inner, basis_edge, inner, edge):
+    first = 0
+    for source in edge_parts:
+        count, _, height = source.shape[:3]
+        pulls.append((source, held.at[first : first + count, :, at : at + height]))
+        first += count
+    pulls = [pltpu.make_async_copy(*pull, in_sems.at[i]) for i, pull in enumerate(pulls)]
+    for pull in pulls:
+        pull.start()
+    lined = jnp.sum(grams[...], axis=0)
+    cols = held.shape[2] // LON
+    gram = jnp.concatenate(
+        [lined[:, cols * p : cols * (p + 1)] for p in range(cols // LON)], axis=0
+    )
+    lhs[...] = frame_rows(frame_of(gram, rank), rank)
+    for pull in pulls:
+        pull.wait()
+
+    step = 2 if levels % 2 == 0 else 1
+
+    def push(i):
+        span = pl.ds(i * step, step)
+        return pltpu.make_async_copy(made.at[:, span], out.at[:, span], out_sems.at[i])
+
+    def project(i, carry):
+        for level in range(step):
+            for f in range(2):
+                both = jnp.dot(
+                    lhs[...], held[i * step + level, f], preferred_element_type=F32
+                )
+                total = both[: rank * LON] + both[rank * LON :]
+                made[:, i * step + level, f] = total.reshape(rank, LON, total.shape[1])
+        push(i).start()
+        return carry
+
+    def finish(i, carry):
+        push(i).wait()
+        return carry
+
+    lax.fori_loop(0, levels // step, project, 0)
+    lax.fori_loop(0, levels // step, finish, 0)
+
+
+def final(grams, basis_inner, basis_edge, inner, edge_parts):
     levels, fields, height, lat = basis_inner.shape
     rank = height // HALF
     cols = rank + inner.shape[2] // HALF
     far = pl.BlockSpec(memory_space=pl.ANY)
+    shape = (rank, levels, fields, LON, lat)
     return pl.pallas_call(
         final_kernel,
-        grid=(levels,),
-        in_specs=[pl.BlockSpec(grams.shape, lambda l: (0, 0, 0)), far, far, far, far],
-        out_specs=pl.BlockSpec((rank, 1, fields, LON, lat), lambda l: (0, l, 0, 0, 0)),
-        out_shape=jax.ShapeDtypeStruct((rank, levels, fields, LON, lat), F32),
+        in_specs=[pl.BlockSpec(memory_space=pltpu.VMEM)] + [far] * (3 + len(edge_parts)),
+        out_specs=far,
+        out_shape=jax.ShapeDtypeStruct(shape, F32),
         scratch_shapes=[
             pltpu.VMEM((2 * rank * LON, cols * LON), BF16),
             pltpu.VMEM((levels, fields, cols * LON, lat), BF16),
-            pltpu.SemaphoreType.DMA((4,)),
+            pltpu.VMEM(shape, F32),
+            pltpu.SemaphoreType.DMA((3 + len(edge_parts),)),
+            pltpu.SemaphoreType.DMA((levels,)),
         ],
         compiler_params=pltpu.CompilerParams(vmem_limit_bytes=40 * MIB),
         name="frame_project",
-    )(grams, basis_inner, basis_edge, inner, edge)
+    )(grams, basis_inner, basis_edge, inner, *edge_parts)
 
 
 def on_device(winds, basis, ground):
@@ -399,9 +457,11 @@
     up_pairs = [(i, (i + 1) % tiles) for i in range(tiles)]
     down_pairs = [(j, i) for i, j in up_pairs]
 
-    up, down = pack(winds)
-    before = lax.ppermute(up, "tile", up_pairs)
-    after = lax.ppermute(down, "tile", down_pairs)
+    spans = spans_of(levels)
+    halos, packed = [], ()
+    for first, count in spans:
+        up, down = packed = pack(winds, first, count, packed)
+        halos.append((lax.ppermute(up, "tile", up_pairs), lax.ppermute(down, "tile", down_pairs)))
 
     cosine = jnp.cos((jnp.arange(lat, dtype=F32) + 0.5) * (jnp.pi / lat) - jnp.pi / 2)
     rows = jnp.stack([cosine, jnp.sqrt(cosine) / cosine / 12.0])
@@ -409,9 +469,12 @@
     ground = ground - lax.axis_index("band") * levels
     ground_edge = jnp.concatenate([ground[6:], ground[:2], ground[6:], ground[:2]])
     part, basis_edge, inner, basis_inner, gram = local(winds, basis, ground, rows)
-    edge, copies = edges(before, after, part, basis_edge, ground_edge, rows, gram, devices)
-    grams = lax.all_to_all(copies, ("band", "tile"), 0, 0)
-    return final(grams, basis_inner, basis_edge, inner, edge)
+    edge_parts = []
+    for (first, count), halo in zip(spans, halos):
+        edge, gram = edges(*halo, part, basis_edge, ground_edge, rows, gram, first, count, devices)
+        edge_parts.append(edge)
+    grams = lax.all_to_all(gram, ("band", "tile"), 0, 0)
+    return final(grams, basis_inner, basis_edge, inner, edge_parts)
 
 
 def solution(mesh):

time: 66.1 us -> 58.9 us (0.89)
  waiting for transfers between devices: 8.87 us -> 0.35 us
  starting transfers between devices: 4.49 us -> 8.19 us
  Pallas kernels: 37.4 us -> 34.9 us
    ppermute x2 -> x4, waiting for transfers between devices: 8.87 us -> 0.35 us  [the longest x2 0.35 us: on_device(): lax.ppermute(down, 'tile', down_pairs)]
    ppermute x2 -> x4, starting transfers between devices: 4.49 us -> 8.19 us  [the longest x2 7.63 us: on_device(): lax.ppermute(down, 'tile', down_pairs)]
    pallas_call x3 -> x5, Pallas kernels: 23.3 us -> 20.8 us  [the longest x1 11.2 us: final(): pl.pallas_call(final_kernel, in_specs=[pl.BlockSpec(memory_space=pltpu.VM...]
  transfers between devices with their start and end apart: 2 -> 4, of which waited for: 2 -> 1; matrix products, arithmetic and copies ran while one was open for 0% -> 1% of each run, Pallas kernels for 21% -> 32%
where the time goes in v2:
time: 58.9 us; the launch traced here: 58.5 us
  Pallas kernels  34.9 us (59%)
  blocking collectives  14.6 us (25%)
  starting transfers between devices  8.19 us (14%)
    all_to_all x1, blocking collectives, on_device(): grams = lax.all_to_all(gram, ('band', 'tile'), 0, 0)  14.6 us
    pallas_call x1, Pallas kernels, local(): pl.pallas_call(local_kernel, grid=(levels,), in_specs=[pl.BlockSpec((fiel...  14.1 us
    pallas_call x1, Pallas kernels, final(): pl.pallas_call(final_kernel, in_specs=[pl.BlockSpec(memory_space=pltpu.VM...  11.2 us
    ppermute x2, starting transfers between devices, on_device(): lax.ppermute(down, 'tile', down_pairs)  7.63 us
    pallas_call x2, Pallas kernels, pack(): pl.pallas_call(functools.partial(pack_kernel, first), in_specs=[pl.BlockS...  5.52 us
    pallas_call x2, Pallas kernels, edges(): pl.pallas_call(functools.partial(edge_kernel, first, last), in_specs=[far...  4.16 us
  transfers between devices with their start and end apart: 4, of which 1 were waited for; matrix products, arithmetic and copies ran while one was open for 1% of the time, Pallas kernels for 32%

profile of v2, /device:TPU:0, one launch (start us, length us, event | category | flops | bytes accessed | tf_op | source)
XLA Modules:
  0.0 58.5 jit_solution(1279038467131999857)
XLA Ops:
  0.0 2.7 %pack_halo.2 = (f32[2,2,2,8,2160]{4,3,2,1,0:T(8,128)}, f32[2,2,2,8,2160]{4,3,2,1,0:T(8,128)}) custom-call(f32[2,8,12,8,720]{4,3,2,1,0:T(8,128)} %winds.5), custom_call_target="tpu_custom_call" | custom-call | tf_op jit(solution)/shard_map/pack_halo/pallas_call | solution.py:86
  2.8 0.0 copy-start
  2.8 0.5 collective-permute-start.2
  3.3 4.1 %collective-permute-start.3 = (f32[2,2,2,8,2160]{4,3,2,1,0:T(8,128)}, f32[2,2,2,8,2160]{4,3,2,1,0:T(8,128)S(1)}, u32[]{:S(2)}, u32[]{:S(2)}) collective-permute-start(f32[2,2,2,8,2160]{4,3,2,1,0:T(8,128)} %get-tuple-element.19.refs_1_), channel_id=1, source_target_pairs={{1,0},{2,1},{3,2},{4,3},{5,4},{6,5},{7,6},{0,7},{9,8},{10,9},{11,1... | collective-permute-start | bytes 1658888 | tf_op jit(solution)/shard_map/ppermute | solution.py:464
  7.4 2.8 %pack_halo.3 = (f32[2,2,2,8,2160]{4,3,2,1,0:T(8,128)}, f32[2,2,2,8,2160]{4,3,2,1,0:T(8,128)}) custom-call(f32[2,8,12,8,720]{4,3,2,1,0:T(8,128)} %winds.5, f32[2,2,2,8,2160]{4,3,2,1,0:T(8,128)} %get-tuple-element.18.refs_0_, f32[2,2,2,8,2160]{4,3,2,1,0:T(8,128)} %get-tuple-element.19.refs_1_), custom_call_target="tpu_custom_call" | custom-call | tf_op jit(solution)/shard_map/pack_halo/pallas_call | solution.py:86
  10.2 0.1 collective-permute-start
  10.2 3.5 %collective-permute-start.1 = (f32[2,2,2,8,2160]{4,3,2,1,0:T(8,128)}, f32[2,2,2,8,2160]{4,3,2,1,0:T(8,128)S(1)}, u32[]{:S(2)}, u32[]{:S(2)}) collective-permute-start(f32[2,2,2,8,2160]{4,3,2,1,0:T(8,128)} %get-tuple-element.21), channel_id=1, source_target_pairs={{1,0},{2,1},{3,2},{4,3},{5,4},{6,5},{7,6},{0,7},{9,8},{10,9},{11,1... | collective-permute-start | bytes 1658888 | tf_op jit(solution)/shard_map/ppermute | solution.py:464
  13.8 0.0 copy-done
  13.8 0.1 fusion
  13.9 0.1 pad.6.clone
  14.0 0.1 maximum_maximum_fusion.rows
  14.1 14.1 %local_stencil.1 = (f32[12,2,32,720]{3,2,1,0:T(8,128)S(1)}, bf16[12,2,96,720]{3,2,1,0:T(8,128)(2,1)S(1)}, bf16[12,2,32,720]{3,2,1,0:T(8,128)(2,1)S(1)}, bf16[12,2,96,720]{3,2,1,0:T(8,128)(2,1)S(1)}, f32[32,32]{1,0:T(8,128)S(1)}) custom-call(f32[2,8,12,8,720]{4,3,2,1,0:T(8,128)} %winds.5, bf16[24,12,2,8,720]{4,3,2,1,0:T(8,128)(2,1)} %basis.1, ...), custom_call_target="tpu_custom_call" | custom-call | flops 2000000000 | bytes 26000000 | tf_op jit(solution)/shard_map/local_stencil/pallas_call | solution.py:198
  28.2 0.0 collective-permute-done.2.before
  28.2 0.0 collective-permute-done.3.after
  28.2 2.0 %edge_gram.2 = (bf16[6,2,32,720]{3,2,1,0:T(8,128)(2,1)S(1)}, f32[32,32]{1,0:T(8,128)S(1)}) custom-call(f32[2,2,2,8,2160]{4,3,2,1,0:T(8,128)S(1)} %collective-permute-done.2.before, f32[2,2,2,8,2160]{4,3,2,1,0:T(8,128)S(1)} %collective-permute-done.3.after, f32[12,2,32,720]{3,2,1,0:T(8,128)S(1)} %get-tuple-element.22.part, ...), custom_call_target="tpu_custom_call" | custom-call | flops 100000000 | bytes 6000000 | tf_op jit(solution)/shard_map/edge_gram/pallas_call | solution.py:291
  30.2 0.0 collective-permute-done.before
  30.2 0.3 collective-permute-done.1.after
  30.6 2.1 %edge_gram.3 = (bf16[6,2,32,720]{3,2,1,0:T(8,128)(2,1)S(1)}, f32[32,8,128]{2,1,0:T(8,128)S(1)}) custom-call(f32[2,2,2,8,2160]{4,3,2,1,0:T(8,128)S(1)} %collective-permute-done.before, f32[2,2,2,8,2160]{4,3,2,1,0:T(8,128)S(1)} %collective-permute-done.1.after, f32[12,2,32,720]{3,2,1,0:T(8,128)S(1)} %get-tuple-element.22.part, ...), custom_call_target="tpu_custom_call" | custom-call | flops 100000000 | bytes 6000000 | tf_op jit(solution)/shard_map/edge_gram/pallas_call | solution.py:291
  32.7 14.6 %all_to_all.5.grams = f32[32,8,128]{2,1,0:T(8,128)S(1)} all-to-all(f32[32,8,128]{2,1,0:T(8,128)S(1)} %get-tuple-element.26), channel_id=1, replica_groups=mesh['band'=4,'tile'=8] {'band','tile'}, dimensions={0} | all-to-all | bytes 262144 | tf_op jit(solution)/shard_map/all_to_all | solution.py:476
  47.3 11.2 %frame_project.1 = f32[24,12,2,8,720]{4,3,2,1,0:T(8,128)} custom-call(f32[32,8,128]{2,1,0:T(8,128)S(1)} %all_to_all.5.grams, bf16[12,2,96,720]{3,2,1,0:T(8,128)(2,1)S(1)} %get-tuple-element.27.basis_inner, bf16[12,2,96,720]{3,2,1,0:T(8,128)(2,1)S(1)} %get-tuple-element.23.basis_edge, bf16[12,2,32,720]{3,2,1,0:T(8,128)(2,1)S(1)} %get-tuple-element.28.inner, ...), custom_call_target="tpu_custom_call" | custom-call | tf_op jit(solution)/shard_map/frame_project/pallas_call | solution.py:436
  (4 shorter events, 0.0 us)
Async XLA Ops:
  2.8 11.0 %copy-start = (s32[8,720]{1,0:T(8,128)S(1)}, s32[8,720]{1,0:T(8,128)}, u32[]{:S(2)}) copy-start(s32[8,720]{1,0:T(8,128)} %param.5) | copy-start | bytes 69124
  2.8 25.4 %collective-permute-start.2 = (f32[2,2,2,8,2160]{4,3,2,1,0:T(8,128)}, f32[2,2,2,8,2160]{4,3,2,1,0:T(8,128)S(1)}, u32[]{:S(2)}, u32[]{:S(2)}) collective-permute-start(f32[2,2,2,8,2160]{4,3,2,1,0:T(8,128)} %get-tuple-element.18.refs_0_), channel_id=1, source_target_pairs={{0,1},{1,2},{2,3},{3,4},{4,5},{5,6},{6,7},{7,0},{8,9},{9,10},{10,1... | collective-permute-start | bytes 1658888 | tf_op jit(solution)/shard_map/ppermute | solution.py:464
  3.3 24.9 %collective-permute-start.3 = (f32[2,2,2,8,2160]{4,3,2,1,0:T(8,128)}, f32[2,2,2,8,2160]{4,3,2,1,0:T(8,128)S(1)}, u32[]{:S(2)}, u32[]{:S(2)}) collective-permute-start(f32[2,2,2,8,2160]{4,3,2,1,0:T(8,128)} %get-tuple-element.19.refs_1_), channel_id=1, source_target_pairs={{1,0},{2,1},{3,2},{4,3},{5,4},{6,5},{7,6},{0,7},{9,8},{10,9},{11,1... | collective-permute-start | bytes 1658888 | tf_op jit(solution)/shard_map/ppermute | solution.py:464
  10.2 20.1 %collective-permute-start = (f32[2,2,2,8,2160]{4,3,2,1,0:T(8,128)}, f32[2,2,2,8,2160]{4,3,2,1,0:T(8,128)S(1)}, u32[]{:S(2)}, u32[]{:S(2)}) collective-permute-start(f32[2,2,2,8,2160]{4,3,2,1,0:T(8,128)} %get-tuple-element.20), channel_id=1, source_target_pairs={{0,1},{1,2},{2,3},{3,4},{4,5},{5,6},{6,7},{7,0},{8,9},{9,10},{10,1... | collective-permute-start | bytes 1658888 | tf_op jit(solution)/shard_map/ppermute | solution.py:464
  10.2 20.4 %collective-permute-start.1 = (f32[2,2,2,8,2160]{4,3,2,1,0:T(8,128)}, f32[2,2,2,8,2160]{4,3,2,1,0:T(8,128)S(1)}, u32[]{:S(2)}, u32[]{:S(2)}) collective-permute-start(f32[2,2,2,8,2160]{4,3,2,1,0:T(8,128)} %get-tuple-element.21), channel_id=1, source_target_pairs={{1,0},{2,1},{3,2},{4,3},{5,4},{6,5},{7,6},{0,7},{9,8},{10,9},{11,1... | collective-permute-start | bytes 1658888 | tf_op jit(solution)/shard_map/ppermute | solution.py:464

commit v3 on v2

--- a/solution.py
+++ b/solution.py
@@ -13,8 +13,8 @@
 HALF = 4
 TURN = 3
 MIB = 1 << 20
-PACK_VMEM = 56 * MIB
-AHEAD = 4
+LEAST_SHARE = 1e-6
+AHEAD = 5
 F32 = jnp.float32
 BF16 = jnp.bfloat16
 
@@ -85,14 +85,15 @@
     whole = pl.BlockSpec(memory_space=pltpu.VMEM)
     return pl.pallas_call(
         functools.partial(pack_kernel, first),
-        in_specs=[pl.BlockSpec(memory_space=pl.ANY)] * (1 + len(after)),
+        in_specs=[pl.BlockSpec(memory_space=pltpu.HBM)]
+        + [pl.BlockSpec(memory_space=pl.ANY)] * len(after),
         out_specs=[whole, whole],
         out_shape=[out, out],
         scratch_shapes=[
             pltpu.VMEM((turns, fields, snaps, turn, lon, lat), F32),
             pltpu.SemaphoreType.DMA((turns,)),
         ],
-        compiler_params=pltpu.CompilerParams(vmem_limit_bytes=PACK_VMEM),
+        compiler_params=pltpu.CompilerParams(vmem_limit_bytes=52 * MIB),
         name="pack_halo",
     )(winds, *after)
 
@@ -219,35 +220,28 @@
 
 
 def edge_kernel(
-    first, last, before, after, part, basis_edge, ground, rows, gram, snap, out, held, acc, sems
+    first, last, before, after, part, basis_edge, ground, rows, gram, snap, out, acc
 ):
     fields, height, lat = part.shape[1:]
     turns, groups = before.shape[1:3]
     turn = snap.shape[0] // turns
     main = whole_lanes(lat)
     rank = gram.shape[0] - height // HALF
-    pulls = []
-    for n in range(turns):
-        for i, source in enumerate((before, after)):
-            pulls.append(pltpu.make_async_copy(source.at[:, n], held.at[i, n], sems.at[i, n]))
-            pulls[-1].start()
     acc[...] = jnp.zeros_like(acc)
     row = rows_of((LON, lat))
     from_after = row % HALF < 2
 
-    def tile(side, n, f, g, i):
+    def tile(halo, n, f, g, i):
         start = turn * main + i * (lat - main)
         return jnp.concatenate(
             [
-                held[side, n, f, g, :, i * main : (i + 1) * main],
-                held[side, n, f, g, :, start : start + lat - main],
+                halo[f, n, g, :, i * main : (i + 1) * main],
+                halo[f, n, g, :, start : start + lat - main],
             ],
             axis=1,
         )
 
     for n in range(turns):
-        pulls[2 * n].wait()
-        pulls[2 * n + 1].wait()
         for i in range(turn):
             here = n * turn + i
             level = first + here
@@ -255,7 +249,7 @@
             for f in range(fields):
                 tiles = []
                 for g in range(groups):
-                    high, low = tile(0, n, 1 - f, g, i), tile(1, n, 1 - f, g, i)
+                    high, low = tile(before, n, 1 - f, g, i), tile(after, n, 1 - f, g, i)
                     tiles.append(jnp.where(from_after, low, high))
                     tiles.append(
                         jnp.where(from_after, pltpu.roll(low, 6, 0), pltpu.roll(high, 2, 0))
@@ -285,22 +279,16 @@
     cols = gram.shape[0]
     last = first + count == levels
     whole = pl.BlockSpec(memory_space=pltpu.VMEM)
-    far = pl.BlockSpec(memory_space=pl.ANY)
-    turns, groups = before.shape[1:3]
     shape = (devices, LON, cols * cols // LON) if last else (cols, cols)
     return pl.pallas_call(
         functools.partial(edge_kernel, first, last),
-        in_specs=[far, far, whole, whole, whole, whole, whole],
+        in_specs=[whole] * 7,
         out_specs=[whole, whole],
         out_shape=[
             jax.ShapeDtypeStruct((count, fields, height, lat), BF16),
             jax.ShapeDtypeStruct(shape, F32),
         ],
-        scratch_shapes=[
-            pltpu.VMEM((2, turns, fields, groups, LON, before.shape[4]), F32),
-            pltpu.VMEM((height, cols * HALF), F32),
-            pltpu.SemaphoreType.DMA((2, turns)),
-        ],
+        scratch_shapes=[pltpu.VMEM((height, cols * HALF), F32)],
         compiler_params=pltpu.CompilerParams(vmem_limit_bytes=32 * MIB),
         cost_estimate=pl.CostEstimate(
             flops=10**8, bytes_accessed=6 * 10**6, transcendentals=0
@@ -319,6 +307,7 @@
 
 def sweep(block, rank):
     lane = lanes_of(block.shape)
+    whole = down_sum(block * block)
     ahead = [spread_lane(block, j) for j in range(AHEAD)]
     for j in range(rank):
         if j + AHEAD < rank:
@@ -329,21 +318,43 @@
         part = jnp.where(lane[:1] > j, down_sum(column * block) * inverse, 0.0)
         block = block - column * part
     norm = down_sum(block * block)
-    return jnp.where(lane < rank, block / jnp.sqrt(norm), 0.0)
-
-
-def frame_of(gram, rank):
-    lane, row = lanes_of(gram.shape), rows_of(gram.shape)
-    frame = sweep(gram, rank)
-    for _ in range(ITERS - 1):
-        frame = sweep(jnp.dot(gram, frame, precision=HIGH, preferred_element_type=F32), rank)
+    share = jnp.where(lane[:1] < rank, norm / whole, 1.0)
+    return jnp.where(lane < rank, block / jnp.sqrt(norm), 0.0), share
+
+
+def times(a, b):
+    return jnp.dot(a, b, precision=HIGH, preferred_element_type=F32)
+
+
+def unit(block, rank):
+    scaled = block * lax.rsqrt(down_sum(block * block))
+    return jnp.where(lanes_of(block.shape) < rank, scaled, 0.0)
+
+
+def once_more(frame, rank):
+    lane, row = lanes_of(frame.shape), rows_of(frame.shape)
     dots = lax.dot_general(
         frame, frame, (((0,), (0,)), ((), ())), precision=HIGH, preferred_element_type=F32
     )
     upper = jnp.where(row < lane, dots, 0.0)
     upper = upper + jnp.where(row == lane, 0.5 * (dots - 1.0), 0.0)
-    upper = jnp.where(lane < rank, upper, 0.0)
-    return frame - jnp.dot(frame, upper, precision=HIGH, preferred_element_type=F32)
+    return frame - times(frame, jnp.where(lane < rank, upper, 0.0))
+
+
+def put_frame(gram, rank, frame_ref):
+    frame, lost = None, jnp.zeros((1, gram.shape[1]), F32)
+    for _ in range(ITERS // 2):
+        frame = gram if frame is None else times(gram, frame)
+        frame, share = sweep(times(gram, unit(frame, rank)), rank)
+        lost = lost + jnp.where(share >= LEAST_SHARE, 0.0, 1.0)
+    frame_ref[...] = once_more(frame, rank)
+
+    @pl.when(jnp.sum(lost) > 0.5)
+    def _():
+        frame, _ = sweep(gram, rank)
+        for _ in range(ITERS - 1):
+            frame, _ = sweep(times(gram, frame), rank)
+        frame_ref[...] = once_more(frame, rank)
 
 
 def frame_rows(frame, rank):
@@ -378,74 +389,69 @@
 
 
 def final_kernel(grams, basis_inner, basis_edge, inner, *refs):
-    edge_parts, (out, lhs, held, made, in_sems, out_sems) = refs[:-6], refs[-6:]
+    edge_parts, (out, frame, lhs, made, sems) = refs[:-5], refs[-5:]
     rank, levels = out.shape[:2]
-    pulls, at = [], 0
-    for source in (basis_inner, basis_edge, inner):
-        height = source.shape[2]
-        pulls.append((source, held.at[:, :, at : at + height]))
-        at += height
-    first = 0
-    for source in edge_parts:
-        count, _, height = source.shape[:3]
-        pulls.append((source, held.at[first : first + count, :, at : at + height]))
-        first += count
-    pulls = [pltpu.make_async_copy(*pull, in_sems.at[i]) for i, pull in enumerate(pulls)]
-    for pull in pulls:
-        pull.start()
     lined = jnp.sum(grams[...], axis=0)
-    cols = held.shape[2] // LON
+    cols = frame.shape[0]
     gram = jnp.concatenate(
         [lined[:, cols * p : cols * (p + 1)] for p in range(cols // LON)], axis=0
     )
-    lhs[...] = frame_rows(frame_of(gram, rank), rank)
-    for pull in pulls:
-        pull.wait()
-
-    step = 2 if levels % 2 == 0 else 1
-
-    def push(i):
-        span = pl.ds(i * step, step)
-        return pltpu.make_async_copy(made.at[:, span], out.at[:, span], out_sems.at[i])
-
-    def project(i, carry):
-        for level in range(step):
-            for f in range(2):
-                both = jnp.dot(
-                    lhs[...], held[i * step + level, f], preferred_element_type=F32
-                )
-                total = both[: rank * LON] + both[rank * LON :]
-                made[:, i * step + level, f] = total.reshape(rank, LON, total.shape[1])
-        push(i).start()
-        return carry
-
-    def finish(i, carry):
-        push(i).wait()
-        return carry
-
-    lax.fori_loop(0, levels // step, project, 0)
-    lax.fori_loop(0, levels // step, finish, 0)
+    put_frame(gram, rank, frame)
+    lhs[...] = frame_rows(frame[...], rank)
+
+    def push(level, count, sem):
+        span = pl.ds(level, count)
+        return pltpu.make_async_copy(made.at[:, span], out.at[:, span], sems.at[sem])
+
+    def project(edge, base, level):
+        for f in range(2):
+            rows = [basis_inner[level, f], basis_edge[level, f], inner[level, f], edge[level - base, f]]
+            both = jnp.dot(
+                lhs[...], jnp.concatenate(rows, axis=0), preferred_element_type=F32
+            )
+            total = both[: rank * LON] + both[rank * LON :]
+            made[:, level, f] = total.reshape(rank, LON, total.shape[1])
+
+    spans, base = [], 0
+    for edge in edge_parts:
+        count = edge.shape[0]
+        alone = 2 - count % 2 if base == 0 else count % 2
+        for level in range(base, base + alone):
+            project(edge, base, level)
+            push(level, 1, level).start()
+            spans.append((level, 1))
+
+        def pair(i, carry, edge=edge, base=base, start=base + alone):
+            level = start + 2 * i
+            project(edge, base, level)
+            project(edge, base, level + 1)
+            push(level, 2, level).start()
+            return carry
+
+        lax.fori_loop(0, (count - alone) // 2, pair, 0)
+        spans += [(level, 2) for level in range(base + alone, base + count, 2)]
+        base += count
+    for level, count in spans:
+        push(level, count, level).wait()
 
 
 def final(grams, basis_inner, basis_edge, inner, edge_parts):
     levels, fields, height, lat = basis_inner.shape
     rank = height // HALF
     cols = rank + inner.shape[2] // HALF
-    far = pl.BlockSpec(memory_space=pl.ANY)
     shape = (rank, levels, fields, LON, lat)
     return pl.pallas_call(
         final_kernel,
-        in_specs=[pl.BlockSpec(memory_space=pltpu.VMEM)] + [far] * (3 + len(edge_parts)),
-        out_specs=far,
+        in_specs=[pl.BlockSpec(memory_space=pltpu.VMEM)] * (4 + len(edge_parts)),
+        out_specs=pl.BlockSpec(memory_space=pltpu.HBM),
         out_shape=jax.ShapeDtypeStruct(shape, F32),
         scratch_shapes=[
+            pltpu.VMEM((cols, cols), F32),
             pltpu.VMEM((2 * rank * LON, cols * LON), BF16),
-            pltpu.VMEM((levels, fields, cols * LON, lat), BF16),
             pltpu.VMEM(shape, F32),
-            pltpu.SemaphoreType.DMA((3 + len(edge_parts),)),
             pltpu.SemaphoreType.DMA((levels,)),
         ],
-        compiler_params=pltpu.CompilerParams(vmem_limit_bytes=40 * MIB),
+        compiler_params=pltpu.CompilerParams(vmem_limit_bytes=32 * MIB),
         name="frame_project",
     )(grams, basis_inner, basis_edge, inner, *edge_parts)
 

time: 58.9 us -> 54.7 us (0.929)
  Pallas kernels: 34.9 us -> 30.2 us
    pallas_call x1, Pallas kernels: 11.2 us -> 8.8 us  [final(): pl.pallas_call(final_kernel, in_specs=[pl.BlockSpec(memory_space=pltpu.VM...]
    pallas_call x2, Pallas kernels: 4.16 us -> 2.68 us  [edges(): pl.pallas_call(functools.partial(edge_kernel, first, last), in_specs=[who...]
    pallas_call x2, Pallas kernels: 5.52 us -> 4.63 us  [pack(): pl.pallas_call(functools.partial(pack_kernel, first), in_specs=[pl.BlockS...]
  transfers between devices with their start and end apart: 4 -> 4, of which waited for: 1 -> 2; matrix products, arithmetic and copies ran while one was open for 1% -> 1% of each run, Pallas kernels for 32% -> 33%
where the time goes in v3:
time: 54.7 us; the launch traced here: 54.3 us
  Pallas kernels  30.2 us (55%)
  blocking collectives  14.6 us (27%)
  starting transfers between devices  8.2 us (15%)
  waiting for transfers between devices  0.93 us (2%)
    all_to_all x1, blocking collectives, on_device(): grams = lax.all_to_all(gram, ('band', 'tile'), 0, 0)  14.6 us
    pallas_call x1, Pallas kernels, local(): pl.pallas_call(local_kernel, grid=(levels,), in_specs=[pl.BlockSpec((fiel...  14.1 us
    pallas_call x1, Pallas kernels, final(): pl.pallas_call(final_kernel, in_specs=[pl.BlockSpec(memory_space=pltpu.VM...  8.8 us
    ppermute x2, starting transfers between devices, on_device(): lax.ppermute(down, 'tile', down_pairs)  7.63 us
    pallas_call x2, Pallas kernels, pack(): pl.pallas_call(functools.partial(pack_kernel, first), in_specs=[pl.BlockS...  4.63 us
    pallas_call x2, Pallas kernels, edges(): pl.pallas_call(functools.partial(edge_kernel, first, last), in_specs=[who...  2.68 us
  transfers between devices with their start and end apart: 4, of which 2 were waited for; matrix products, arithmetic and copies ran while one was open for 1% of the time, Pallas kernels for 33%

profile of v3, /device:TPU:0, one launch (start us, length us, event | category | flops | bytes accessed | tf_op | source)
XLA Modules:
  0.0 54.3 jit_solution(16269469115370449117)
XLA Ops:
  0.0 1.9 %pack_halo.2 = (f32[2,2,2,8,2160]{4,3,2,1,0:T(8,128)S(1)}, f32[2,2,2,8,2160]{4,3,2,1,0:T(8,128)S(1)}) custom-call(f32[2,8,12,8,720]{4,3,2,1,0:T(8,128)} %winds.5), custom_call_target="tpu_custom_call" | custom-call | tf_op jit(solution)/shard_map/pack_halo/pallas_call | solution.py:86
  1.9 0.0 copy-start
  1.9 0.0 copy-start.1
  1.9 0.5 collective-permute-start.2
  2.4 4.1 %collective-permute-start.3 = (f32[2,2,2,8,2160]{4,3,2,1,0:T(8,128)S(1)}, f32[2,2,2,8,2160]{4,3,2,1,0:T(8,128)S(1)}, u32[]{:S(2)}, u32[]{:S(2)}) collective-permute-start(f32[2,2,2,8,2160]{4,3,2,1,0:T(8,128)S(1)} %get-tuple-element.19.refs_1_), channel_id=1, source_target_pairs={{1,0},{2,1},{3,2},{4,3},{5,4},{6,5},{7,6},{0,7},{9,8},{10,9},{11,1... | collective-permute-start | bytes 1658888 | tf_op jit(solution)/shard_map/ppermute | solution.py:470
  6.5 0.0 copy-done
  6.5 2.8 %pack_halo.3 = (f32[2,2,2,8,2160]{4,3,2,1,0:T(8,128)}, f32[2,2,2,8,2160]{4,3,2,1,0:T(8,128)}) custom-call(f32[2,8,12,8,720]{4,3,2,1,0:T(8,128)} %winds.5, f32[2,2,2,8,2160]{4,3,2,1,0:T(8,128)S(1)} %get-tuple-element.18.refs_0_, f32[2,2,2,8,2160]{4,3,2,1,0:T(8,128)} %copy-done), custom_call_target="tpu_custom_call" | custom-call | tf_op jit(solution)/shard_map/pack_halo/pallas_call | solution.py:86
  9.3 0.1 collective-permute-start
  9.3 3.5 %collective-permute-start.1 = (f32[2,2,2,8,2160]{4,3,2,1,0:T(8,128)}, f32[2,2,2,8,2160]{4,3,2,1,0:T(8,128)S(1)}, u32[]{:S(2)}, u32[]{:S(2)}) collective-permute-start(f32[2,2,2,8,2160]{4,3,2,1,0:T(8,128)} %get-tuple-element.21), channel_id=1, source_target_pairs={{1,0},{2,1},{3,2},{4,3},{5,4},{6,5},{7,6},{0,7},{9,8},{10,9},{11,1... | collective-permute-start | bytes 1658888 | tf_op jit(solution)/shard_map/ppermute | solution.py:470
  12.9 0.0 copy-done.1
  12.9 0.1 fusion
  13.0 0.1 pad.6.clone
  13.1 0.1 maximum_maximum_fusion.rows
  13.2 14.1 %local_stencil.1 = (f32[12,2,32,720]{3,2,1,0:T(8,128)S(1)}, bf16[12,2,96,720]{3,2,1,0:T(8,128)(2,1)S(1)}, bf16[12,2,32,720]{3,2,1,0:T(8,128)(2,1)S(1)}, bf16[12,2,96,720]{3,2,1,0:T(8,128)(2,1)S(1)}, f32[32,32]{1,0:T(8,128)S(1)}) custom-call(f32[2,8,12,8,720]{4,3,2,1,0:T(8,128)} %winds.5, bf16[24,12,2,8,720]{4,3,2,1,0:T(8,128)(2,1)} %basis.1, ...), custom_call_target="tpu_custom_call" | custom-call | flops 2000000000 | bytes 26000000 | tf_op jit(solution)/shard_map/local_stencil/pallas_call | solution.py:199
  27.3 0.0 collective-permute-done.2.before
  27.3 0.0 collective-permute-done.3.after
  27.3 1.3 %edge_gram.2 = (bf16[6,2,32,720]{3,2,1,0:T(8,128)(2,1)S(1)}, f32[32,32]{1,0:T(8,128)S(1)}) custom-call(f32[2,2,2,8,2160]{4,3,2,1,0:T(8,128)S(1)} %collective-permute-done.2.before, f32[2,2,2,8,2160]{4,3,2,1,0:T(8,128)S(1)} %collective-permute-done.3.after, f32[12,2,32,720]{3,2,1,0:T(8,128)S(1)} %get-tuple-element.22.part, ...), custom_call_target="tpu_custom_call" | custom-call | flops 100000000 | bytes 6000000 | tf_op jit(solution)/shard_map/edge_gram/pallas_call | solution.py:283
  28.6 0.3 collective-permute-done.before
  28.9 0.6 %collective-permute-done.1.after = f32[2,2,2,8,2160]{4,3,2,1,0:T(8,128)S(1)} collective-permute-done((f32[2,2,2,8,2160]{4,3,2,1,0:T(8,128)}, f32[2,2,2,8,2160]{4,3,2,1,0:T(8,128)S(1)}, u32[]{:S(2)}, u32[]{:S(2)}) %collective-permute-start.1) | collective-permute-done | bytes 552992 | tf_op jit(solution)/shard_map/ppermute | solution.py:470
  29.5 1.4 %edge_gram.3 = (bf16[6,2,32,720]{3,2,1,0:T(8,128)(2,1)S(1)}, f32[32,8,128]{2,1,0:T(8,128)S(1)}) custom-call(f32[2,2,2,8,2160]{4,3,2,1,0:T(8,128)S(1)} %collective-permute-done.before, f32[2,2,2,8,2160]{4,3,2,1,0:T(8,128)S(1)} %collective-permute-done.1.after, f32[12,2,32,720]{3,2,1,0:T(8,128)S(1)} %get-tuple-element.22.part, ...), custom_call_target="tpu_custom_call" | custom-call | flops 100000000 | bytes 6000000 | tf_op jit(solution)/shard_map/edge_gram/pallas_call | solution.py:283
  30.9 14.6 %all_to_all.5.grams = f32[32,8,128]{2,1,0:T(8,128)S(1)} all-to-all(f32[32,8,128]{2,1,0:T(8,128)S(1)} %get-tuple-element.26), channel_id=1, replica_groups=mesh['band'=4,'tile'=8] {'band','tile'}, dimensions={0} | all-to-all | bytes 262144 | tf_op jit(solution)/shard_map/all_to_all | solution.py:482
  45.5 8.8 %frame_project.1 = f32[24,12,2,8,720]{4,3,2,1,0:T(8,128)} custom-call(f32[32,8,128]{2,1,0:T(8,128)S(1)} %all_to_all.5.grams, bf16[12,2,96,720]{3,2,1,0:T(8,128)(2,1)S(1)} %get-tuple-element.27.basis_inner, bf16[12,2,96,720]{3,2,1,0:T(8,128)(2,1)S(1)} %get-tuple-element.23.basis_edge, bf16[12,2,32,720]{3,2,1,0:T(8,128)(2,1)S(1)} %get-tuple-element.28.inner, ...), custom_call_target="tpu_custom_call" | custom-call | tf_op jit(solution)/shard_map/frame_project/pallas_call | solution.py:443
  (4 shorter events, 0.0 us)
Async XLA Ops:
  1.9 4.6 %copy-start = (f32[2,2,2,8,2160]{4,3,2,1,0:T(8,128)}, f32[2,2,2,8,2160]{4,3,2,1,0:T(8,128)S(1)}, u32[]{:S(2)}) copy-start(f32[2,2,2,8,2160]{4,3,2,1,0:T(8,128)S(1)} %get-tuple-element.19.refs_1_) | copy-start | bytes 1658884
  1.9 11.0 %copy-start.1 = (s32[8,720]{1,0:T(8,128)S(1)}, s32[8,720]{1,0:T(8,128)}, u32[]{:S(2)}) copy-start(s32[8,720]{1,0:T(8,128)} %param.5) | copy-start | bytes 69124
  1.9 25.4 %collective-permute-start.2 = (f32[2,2,2,8,2160]{4,3,2,1,0:T(8,128)S(1)}, f32[2,2,2,8,2160]{4,3,2,1,0:T(8,128)S(1)}, u32[]{:S(2)}, u32[]{:S(2)}) collective-permute-start(f32[2,2,2,8,2160]{4,3,2,1,0:T(8,128)S(1)} %get-tuple-element.18.refs_0_), channel_id=1, source_target_pairs={{0,1},{1,2},{2,3},{3,4},{4,5},{5,6},{6,7},{7,0},{8,9},{9,10},{10,1... | collective-permute-start | bytes 1658888 | tf_op jit(solution)/shard_map/ppermute | solution.py:470
  2.4 24.9 %collective-permute-start.3 = (f32[2,2,2,8,2160]{4,3,2,1,0:T(8,128)S(1)}, f32[2,2,2,8,2160]{4,3,2,1,0:T(8,128)S(1)}, u32[]{:S(2)}, u32[]{:S(2)}) collective-permute-start(f32[2,2,2,8,2160]{4,3,2,1,0:T(8,128)S(1)} %get-tuple-element.19.refs_1_), channel_id=1, source_target_pairs={{1,0},{2,1},{3,2},{4,3},{5,4},{6,5},{7,6},{0,7},{9,8},{10,9},{11,1... | collective-permute-start | bytes 1658888 | tf_op jit(solution)/shard_map/ppermute | solution.py:470
  9.3 19.6 %collective-permute-start = (f32[2,2,2,8,2160]{4,3,2,1,0:T(8,128)}, f32[2,2,2,8,2160]{4,3,2,1,0:T(8,128)S(1)}, u32[]{:S(2)}, u32[]{:S(2)}) collective-permute-start(f32[2,2,2,8,2160]{4,3,2,1,0:T(8,128)} %get-tuple-element.20), channel_id=1, source_target_pairs={{0,1},{1,2},{2,3},{3,4},{4,5},{5,6},{6,7},{7,0},{8,9},{9,10},{10,1... | collective-permute-start | bytes 1658888 | tf_op jit(solution)/shard_map/ppermute | solution.py:470
  9.3 20.2 %collective-permute-start.1 = (f32[2,2,2,8,2160]{4,3,2,1,0:T(8,128)}, f32[2,2,2,8,2160]{4,3,2,1,0:T(8,128)S(1)}, u32[]{:S(2)}, u32[]{:S(2)}) collective-permute-start(f32[2,2,2,8,2160]{4,3,2,1,0:T(8,128)} %get-tuple-element.21), channel_id=1, source_target_pairs={{1,0},{2,1},{3,2},{4,3},{5,4},{6,5},{7,6},{0,7},{9,8},{10,9},{11,1... | collective-permute-start | bytes 1658888 | tf_op jit(solution)/shard_map/ppermute | solution.py:470

commit v4 on v3

--- a/solution.py
+++ b/solution.py
@@ -399,40 +399,26 @@
     put_frame(gram, rank, frame)
     lhs[...] = frame_rows(frame[...], rank)
 
-    def push(level, count, sem):
-        span = pl.ds(level, count)
-        return pltpu.make_async_copy(made.at[:, span], out.at[:, span], sems.at[sem])
+    def push(level):
+        return pltpu.make_async_copy(made.at[:, level], out.at[:, level], sems.at[level])
 
     def project(edge, base, level):
         for f in range(2):
-            rows = [basis_inner[level, f], basis_edge[level, f], inner[level, f], edge[level - base, f]]
-            both = jnp.dot(
-                lhs[...], jnp.concatenate(rows, axis=0), preferred_element_type=F32
-            )
+            rows = [source[level, f] for source in (basis_inner, basis_edge, inner)]
+            rows = jnp.concatenate(rows + [edge[level - base, f]], axis=0)
+            both = jnp.dot(lhs[...], rows, preferred_element_type=F32)
             total = both[: rank * LON] + both[rank * LON :]
             made[:, level, f] = total.reshape(rank, LON, total.shape[1])
 
-    spans, base = [], 0
+    pushes, base = [], 0
     for edge in edge_parts:
-        count = edge.shape[0]
-        alone = 2 - count % 2 if base == 0 else count % 2
-        for level in range(base, base + alone):
+        for level in range(base, base + edge.shape[0]):
             project(edge, base, level)
-            push(level, 1, level).start()
-            spans.append((level, 1))
-
-        def pair(i, carry, edge=edge, base=base, start=base + alone):
-            level = start + 2 * i
-            project(edge, base, level)
-            project(edge, base, level + 1)
-            push(level, 2, level).start()
-            return carry
-
-        lax.fori_loop(0, (count - alone) // 2, pair, 0)
-        spans += [(level, 2) for level in range(base + alone, base + count, 2)]
-        base += count
-    for level, count in spans:
-        push(level, count, level).wait()
+            pushes.append(push(level))
+            pushes[-1].start()
+        base += edge.shape[0]
+    for copy in pushes:
+        copy.wait()
 
 
 def final(grams, basis_inner, basis_edge, inner, edge_parts):

time: 54.7 us -> 54.1 us (0.989)
  Pallas kernels: 30.2 us -> 29.6 us
    pallas_call x1, Pallas kernels: 8.8 us -> 8.21 us  [final(): pl.pallas_call(final_kernel, in_specs=[pl.BlockSpec(memory_space=pltpu.VM...]
  transfers between devices with their start and end apart: 4 -> 4, of which waited for: 2 -> 2; matrix products, arithmetic and copies ran while one was open for 1% -> 1% of each run, Pallas kernels for 33% -> 34%
where the time goes in v4:
time: 54.1 us; the launch traced here: 53.7 us
  Pallas kernels  29.6 us (55%)
  blocking collectives  14.6 us (27%)
  starting transfers between devices  8.2 us (15%)
  waiting for transfers between devices  0.93 us (2%)
    all_to_all x1, blocking collectives, on_device(): grams = lax.all_to_all(gram, ('band', 'tile'), 0, 0)  14.6 us
    pallas_call x1, Pallas kernels, local(): pl.pallas_call(local_kernel, grid=(levels,), in_specs=[pl.BlockSpec((fiel...  14.1 us
    pallas_call x1, Pallas kernels, final(): pl.pallas_call(final_kernel, in_specs=[pl.BlockSpec(memory_space=pltpu.VM...  8.21 us
    ppermute x2, starting transfers between devices, on_device(): lax.ppermute(down, 'tile', down_pairs)  7.63 us
    pallas_call x2, Pallas kernels, pack(): pl.pallas_call(functools.partial(pack_kernel, first), in_specs=[pl.BlockS...  4.63 us
    pallas_call x2, Pallas kernels, edges(): pl.pallas_call(functools.partial(edge_kernel, first, last), in_specs=[who...  2.68 us
  transfers between devices with their start and end apart: 4, of which 2 were waited for; matrix products, arithmetic and copies ran while one was open for 1% of the time, Pallas kernels for 34%

profile of v4, /device:TPU:0, one launch (start us, length us, event | category | flops | bytes accessed | tf_op | source)
XLA Modules:
  0.0 53.7 jit_solution(8781436999598480964)
XLA Ops:
  0.0 1.9 %pack_halo.2 = (f32[2,2,2,8,2160]{4,3,2,1,0:T(8,128)S(1)}, f32[2,2,2,8,2160]{4,3,2,1,0:T(8,128)S(1)}) custom-call(f32[2,8,12,8,720]{4,3,2,1,0:T(8,128)} %winds.5), custom_call_target="tpu_custom_call" | custom-call | tf_op jit(solution)/shard_map/pack_halo/pallas_call | solution.py:86
  1.9 0.0 copy-start
  1.9 0.0 copy-start.1
  1.9 0.5 collective-permute-start.2
  2.4 4.1 %collective-permute-start.3 = (f32[2,2,2,8,2160]{4,3,2,1,0:T(8,128)S(1)}, f32[2,2,2,8,2160]{4,3,2,1,0:T(8,128)S(1)}, u32[]{:S(2)}, u32[]{:S(2)}) collective-permute-start(f32[2,2,2,8,2160]{4,3,2,1,0:T(8,128)S(1)} %get-tuple-element.19.refs_1_), channel_id=1, source_target_pairs={{1,0},{2,1},{3,2},{4,3},{5,4},{6,5},{7,6},{0,7},{9,8},{10,9},{11,1... | collective-permute-start | bytes 1658888 | tf_op jit(solution)/shard_map/ppermute | solution.py:456
  6.5 0.0 copy-done
  6.5 2.8 %pack_halo.3 = (f32[2,2,2,8,2160]{4,3,2,1,0:T(8,128)}, f32[2,2,2,8,2160]{4,3,2,1,0:T(8,128)}) custom-call(f32[2,8,12,8,720]{4,3,2,1,0:T(8,128)} %winds.5, f32[2,2,2,8,2160]{4,3,2,1,0:T(8,128)S(1)} %get-tuple-element.18.refs_0_, f32[2,2,2,8,2160]{4,3,2,1,0:T(8,128)} %copy-done), custom_call_target="tpu_custom_call" | custom-call | tf_op jit(solution)/shard_map/pack_halo/pallas_call | solution.py:86
  9.3 0.1 collective-permute-start
  9.3 3.5 %collective-permute-start.1 = (f32[2,2,2,8,2160]{4,3,2,1,0:T(8,128)}, f32[2,2,2,8,2160]{4,3,2,1,0:T(8,128)S(1)}, u32[]{:S(2)}, u32[]{:S(2)}) collective-permute-start(f32[2,2,2,8,2160]{4,3,2,1,0:T(8,128)} %get-tuple-element.21), channel_id=1, source_target_pairs={{1,0},{2,1},{3,2},{4,3},{5,4},{6,5},{7,6},{0,7},{9,8},{10,9},{11,1... | collective-permute-start | bytes 1658888 | tf_op jit(solution)/shard_map/ppermute | solution.py:456
  12.9 0.0 copy-done.1
  12.9 0.1 fusion
  13.0 0.1 pad.6.clone
  13.1 0.1 maximum_maximum_fusion.rows
  13.2 14.1 %local_stencil.1 = (f32[12,2,32,720]{3,2,1,0:T(8,128)S(1)}, bf16[12,2,96,720]{3,2,1,0:T(8,128)(2,1)S(1)}, bf16[12,2,32,720]{3,2,1,0:T(8,128)(2,1)S(1)}, bf16[12,2,96,720]{3,2,1,0:T(8,128)(2,1)S(1)}, f32[32,32]{1,0:T(8,128)S(1)}) custom-call(f32[2,8,12,8,720]{4,3,2,1,0:T(8,128)} %winds.5, bf16[24,12,2,8,720]{4,3,2,1,0:T(8,128)(2,1)} %basis.1, ...), custom_call_target="tpu_custom_call" | custom-call | flops 2000000000 | bytes 26000000 | tf_op jit(solution)/shard_map/local_stencil/pallas_call | solution.py:199
  27.3 0.0 collective-permute-done.2.before
  27.3 0.0 collective-permute-done.3.after
  27.3 1.3 %edge_gram.2 = (bf16[6,2,32,720]{3,2,1,0:T(8,128)(2,1)S(1)}, f32[32,32]{1,0:T(8,128)S(1)}) custom-call(f32[2,2,2,8,2160]{4,3,2,1,0:T(8,128)S(1)} %collective-permute-done.2.before, f32[2,2,2,8,2160]{4,3,2,1,0:T(8,128)S(1)} %collective-permute-done.3.after, f32[12,2,32,720]{3,2,1,0:T(8,128)S(1)} %get-tuple-element.22.part, ...), custom_call_target="tpu_custom_call" | custom-call | flops 100000000 | bytes 6000000 | tf_op jit(solution)/shard_map/edge_gram/pallas_call | solution.py:283
  28.6 0.3 collective-permute-done.before
  28.9 0.6 %collective-permute-done.1.after = f32[2,2,2,8,2160]{4,3,2,1,0:T(8,128)S(1)} collective-permute-done((f32[2,2,2,8,2160]{4,3,2,1,0:T(8,128)}, f32[2,2,2,8,2160]{4,3,2,1,0:T(8,128)S(1)}, u32[]{:S(2)}, u32[]{:S(2)}) %collective-permute-start.1) | collective-permute-done | bytes 552992 | tf_op jit(solution)/shard_map/ppermute | solution.py:456
  29.5 1.4 %edge_gram.3 = (bf16[6,2,32,720]{3,2,1,0:T(8,128)(2,1)S(1)}, f32[32,8,128]{2,1,0:T(8,128)S(1)}) custom-call(f32[2,2,2,8,2160]{4,3,2,1,0:T(8,128)S(1)} %collective-permute-done.before, f32[2,2,2,8,2160]{4,3,2,1,0:T(8,128)S(1)} %collective-permute-done.1.after, f32[12,2,32,720]{3,2,1,0:T(8,128)S(1)} %get-tuple-element.22.part, ...), custom_call_target="tpu_custom_call" | custom-call | flops 100000000 | bytes 6000000 | tf_op jit(solution)/shard_map/edge_gram/pallas_call | solution.py:283
  30.9 14.6 %all_to_all.5.grams = f32[32,8,128]{2,1,0:T(8,128)S(1)} all-to-all(f32[32,8,128]{2,1,0:T(8,128)S(1)} %get-tuple-element.26), channel_id=1, replica_groups=mesh['band'=4,'tile'=8] {'band','tile'}, dimensions={0} | all-to-all | bytes 262144 | tf_op jit(solution)/shard_map/all_to_all | solution.py:468
  45.5 8.2 %frame_project.1 = f32[24,12,2,8,720]{4,3,2,1,0:T(8,128)} custom-call(f32[32,8,128]{2,1,0:T(8,128)S(1)} %all_to_all.5.grams, bf16[12,2,96,720]{3,2,1,0:T(8,128)(2,1)S(1)} %get-tuple-element.27.basis_inner, bf16[12,2,96,720]{3,2,1,0:T(8,128)(2,1)S(1)} %get-tuple-element.23.basis_edge, bf16[12,2,32,720]{3,2,1,0:T(8,128)(2,1)S(1)} %get-tuple-element.28.inner, ...), custom_call_target="tpu_custom_call" | custom-call | tf_op jit(solution)/shard_map/frame_project/pallas_call | solution.py:429
  (4 shorter events, 0.0 us)
Async XLA Ops:
  1.9 4.6 %copy-start = (f32[2,2,2,8,2160]{4,3,2,1,0:T(8,128)}, f32[2,2,2,8,2160]{4,3,2,1,0:T(8,128)S(1)}, u32[]{:S(2)}) copy-start(f32[2,2,2,8,2160]{4,3,2,1,0:T(8,128)S(1)} %get-tuple-element.19.refs_1_) | copy-start | bytes 1658884
  1.9 11.0 %copy-start.1 = (s32[8,720]{1,0:T(8,128)S(1)}, s32[8,720]{1,0:T(8,128)}, u32[]{:S(2)}) copy-start(s32[8,720]{1,0:T(8,128)} %param.5) | copy-start | bytes 69124
  1.9 25.4 %collective-permute-start.2 = (f32[2,2,2,8,2160]{4,3,2,1,0:T(8,128)S(1)}, f32[2,2,2,8,2160]{4,3,2,1,0:T(8,128)S(1)}, u32[]{:S(2)}, u32[]{:S(2)}) collective-permute-start(f32[2,2,2,8,2160]{4,3,2,1,0:T(8,128)S(1)} %get-tuple-element.18.refs_0_), channel_id=1, source_target_pairs={{0,1},{1,2},{2,3},{3,4},{4,5},{5,6},{6,7},{7,0},{8,9},{9,10},{10,1... | collective-permute-start | bytes 1658888 | tf_op jit(solution)/shard_map/ppermute | solution.py:456
  2.4 24.9 %collective-permute-start.3 = (f32[2,2,2,8,2160]{4,3,2,1,0:T(8,128)S(1)}, f32[2,2,2,8,2160]{4,3,2,1,0:T(8,128)S(1)}, u32[]{:S(2)}, u32[]{:S(2)}) collective-permute-start(f32[2,2,2,8,2160]{4,3,2,1,0:T(8,128)S(1)} %get-tuple-element.19.refs_1_), channel_id=1, source_target_pairs={{1,0},{2,1},{3,2},{4,3},{5,4},{6,5},{7,6},{0,7},{9,8},{10,9},{11,1... | collective-permute-start | bytes 1658888 | tf_op jit(solution)/shard_map/ppermute | solution.py:456
  9.3 19.6 %collective-permute-start = (f32[2,2,2,8,2160]{4,3,2,1,0:T(8,128)}, f32[2,2,2,8,2160]{4,3,2,1,0:T(8,128)S(1)}, u32[]{:S(2)}, u32[]{:S(2)}) collective-permute-start(f32[2,2,2,8,2160]{4,3,2,1,0:T(8,128)} %get-tuple-element.20), channel_id=1, source_target_pairs={{0,1},{1,2},{2,3},{3,4},{4,5},{5,6},{6,7},{7,0},{8,9},{9,10},{10,1... | collective-permute-start | bytes 1658888 | tf_op jit(solution)/shard_map/ppermute | solution.py:456
  9.3 20.2 %collective-permute-start.1 = (f32[2,2,2,8,2160]{4,3,2,1,0:T(8,128)}, f32[2,2,2,8,2160]{4,3,2,1,0:T(8,128)S(1)}, u32[]{:S(2)}, u32[]{:S(2)}) collective-permute-start(f32[2,2,2,8,2160]{4,3,2,1,0:T(8,128)} %get-tuple-element.21), channel_id=1, source_target_pairs={{1,0},{2,1},{3,2},{4,3},{5,4},{6,5},{7,6},{0,7},{9,8},{10,9},{11,1... | collective-permute-start | bytes 1658888 | tf_op jit(solution)/shard_map/ppermute | solution.py:456

commit v5 on v4

--- a/solution.py
+++ b/solution.py
@@ -41,34 +41,34 @@
     return lat // 128 * 128
 
 
-def ordered(row, at2, at4, at6, rest):
-    return jnp.where(row < 2, at2, jnp.where(row < 4, at4, jnp.where(row < 6, at6, rest)))
-
-
 def pack_kernel(first, winds, *refs):
     up, down, held, sems = refs[-4:]
     fields, snaps = winds.shape[:2]
-    turns, turn = held.shape[0], held.shape[3]
-    lat = winds.shape[4]
+    turns, turn, lat = held.shape[0], held.shape[4], held.shape[6]
     main = whole_lanes(lat)
     pulls = []
     for n in range(turns):
         levels = pl.ds(first + n * turn, turn)
-        pulls.append(pltpu.make_async_copy(winds.at[:, :, levels], held.at[n], sems.at[n]))
-        pulls[-1].start()
-    row = rows_of((LON, lat))
-    odd = row % 2 == 1
+        for side, lon in enumerate((0, LON - 2)):
+            pulls.append(
+                pltpu.make_async_copy(
+                    winds.at[:, :, levels, lon : lon + 2], held.at[n, side], sems.at[n, side]
+                )
+            )
+            pulls[-1].start()
+    odd = rows_of((LON, lat)) % 2 == 1
     for n in range(turns):
-        pulls[n].wait()
+        pulls[2 * n].wait()
+        pulls[2 * n + 1].wait()
         for f in range(fields):
             for g in range(snaps // 4):
                 tails = ([], [])
                 for i in range(turn):
-                    x = [held[n, f, 4 * g + t, i] for t in range(4)]
-                    both2, both6 = pltpu.roll(x[2], 2, 0), pltpu.roll(x[3], 6, 0)
-                    low = ordered(row, x[0], both2, pltpu.roll(x[1], 4, 0), both6)
+                    low = [held[n, 0, f, 4 * g + t, i] for t in (0, 2, 1, 3)]
+                    low = jnp.concatenate(low, axis=0)
                     low = jnp.where(odd, 8.0 * pltpu.roll(low, 1, 0), 0.0) - low
-                    high = ordered(row, both2, pltpu.roll(x[0], 4, 0), both6, x[1])
+                    high = [held[n, 1, f, 4 * g + t, i] for t in (2, 0, 3, 1)]
+                    high = jnp.concatenate(high, axis=0)
                     high = high - jnp.where(odd, 0.0, 8.0 * pltpu.roll(high, 7, 0))
                     for ref, tail, tile in ((down, tails[0], low), (up, tails[1], high)):
                         ref[f, n, g, :, i * main : (i + 1) * main] = tile[:, :main]
@@ -90,8 +90,8 @@
         out_specs=[whole, whole],
         out_shape=[out, out],
         scratch_shapes=[
-            pltpu.VMEM((turns, fields, snaps, turn, lon, lat), F32),
-            pltpu.SemaphoreType.DMA((turns,)),
+            pltpu.VMEM((turns, 2, fields, snaps, turn, 2, lat), F32),
+            pltpu.SemaphoreType.DMA((turns, 2)),
         ],
         compiler_params=pltpu.CompilerParams(vmem_limit_bytes=52 * MIB),
         name="pack_halo",

time: 54.1 us -> 53.9 us (level)
  transfers between devices with their start and end apart: 4 -> 4, of which waited for: 2 -> 2; matrix products, arithmetic and copies ran while one was open for 1% -> 1% of each run, Pallas kernels for 34% -> 33%
where the time goes in v5:
time: 53.9 us; the launch traced here: 53.5 us
  Pallas kernels  29.1 us (54%)
  blocking collectives  14.6 us (27%)
  starting transfers between devices  8.2 us (15%)
  waiting for transfers between devices  1.17 us (2%)
    all_to_all x1, blocking collectives, on_device(): grams = lax.all_to_all(gram, ('band', 'tile'), 0, 0)  14.6 us
    pallas_call x1, Pallas kernels, local(): pl.pallas_call(local_kernel, grid=(levels,), in_specs=[pl.BlockSpec((fiel...  14.1 us
    pallas_call x1, Pallas kernels, final(): pl.pallas_call(final_kernel, in_specs=[pl.BlockSpec(memory_space=pltpu.VM...  8.21 us
    ppermute x2, starting transfers between devices, on_device(): lax.ppermute(down, 'tile', down_pairs)  7.63 us
    pallas_call x2, Pallas kernels, pack(): pl.pallas_call(functools.partial(pack_kernel, first), in_specs=[pl.BlockS...  4.14 us
    pallas_call x2, Pallas kernels, edges(): pl.pallas_call(functools.partial(edge_kernel, first, last), in_specs=[who...  2.68 us
  transfers between devices with their start and end apart: 4, of which 2 were waited for; matrix products, arithmetic and copies ran while one was open for 1% of the time, Pallas kernels for 33%

profile of v5, /device:TPU:0, one launch (start us, length us, event | category | flops | bytes accessed | tf_op | source)
XLA Modules:
  0.0 53.5 jit_solution(16540640944362169810)
XLA Ops:
  0.0 1.6 %pack_halo.2 = (f32[2,2,2,8,2160]{4,3,2,1,0:T(8,128)S(1)}, f32[2,2,2,8,2160]{4,3,2,1,0:T(8,128)S(1)}) custom-call(f32[2,8,12,8,720]{4,3,2,1,0:T(8,128)} %winds.5), custom_call_target="tpu_custom_call" | custom-call | tf_op jit(solution)/shard_map/pack_halo/pallas_call | solution.py:86
  1.6 0.0 copy-start
  1.7 0.0 copy-start.1
  1.7 0.5 collective-permute-start.2
  2.2 4.1 %collective-permute-start.3 = (f32[2,2,2,8,2160]{4,3,2,1,0:T(8,128)S(1)}, f32[2,2,2,8,2160]{4,3,2,1,0:T(8,128)S(1)}, u32[]{:S(2)}, u32[]{:S(2)}) collective-permute-start(f32[2,2,2,8,2160]{4,3,2,1,0:T(8,128)S(1)} %get-tuple-element.19.refs_1_), channel_id=1, source_target_pairs={{1,0},{2,1},{3,2},{4,3},{5,4},{6,5},{7,6},{0,7},{9,8},{10,9},{11,1... | collective-permute-start | bytes 1658888 | tf_op jit(solution)/shard_map/ppermute | solution.py:456
  6.3 0.0 copy-done
  6.3 2.5 %pack_halo.3 = (f32[2,2,2,8,2160]{4,3,2,1,0:T(8,128)}, f32[2,2,2,8,2160]{4,3,2,1,0:T(8,128)}) custom-call(f32[2,8,12,8,720]{4,3,2,1,0:T(8,128)} %winds.5, f32[2,2,2,8,2160]{4,3,2,1,0:T(8,128)S(1)} %get-tuple-element.18.refs_0_, f32[2,2,2,8,2160]{4,3,2,1,0:T(8,128)} %copy-done), custom_call_target="tpu_custom_call" | custom-call | tf_op jit(solution)/shard_map/pack_halo/pallas_call | solution.py:86
  8.8 0.1 collective-permute-start
  8.9 3.5 %collective-permute-start.1 = (f32[2,2,2,8,2160]{4,3,2,1,0:T(8,128)}, f32[2,2,2,8,2160]{4,3,2,1,0:T(8,128)S(1)}, u32[]{:S(2)}, u32[]{:S(2)}) collective-permute-start(f32[2,2,2,8,2160]{4,3,2,1,0:T(8,128)} %get-tuple-element.21), channel_id=1, source_target_pairs={{1,0},{2,1},{3,2},{4,3},{5,4},{6,5},{7,6},{0,7},{9,8},{10,9},{11,1... | collective-permute-start | bytes 1658888 | tf_op jit(solution)/shard_map/ppermute | solution.py:456
  12.4 0.0 copy-done.1
  12.4 0.1 fusion
  12.5 0.1 pad.6.clone
  12.6 0.1 maximum_maximum_fusion.rows
  12.7 14.1 %local_stencil.1 = (f32[12,2,32,720]{3,2,1,0:T(8,128)S(1)}, bf16[12,2,96,720]{3,2,1,0:T(8,128)(2,1)S(1)}, bf16[12,2,32,720]{3,2,1,0:T(8,128)(2,1)S(1)}, bf16[12,2,96,720]{3,2,1,0:T(8,128)(2,1)S(1)}, f32[32,32]{1,0:T(8,128)S(1)}) custom-call(f32[2,8,12,8,720]{4,3,2,1,0:T(8,128)} %winds.5, bf16[24,12,2,8,720]{4,3,2,1,0:T(8,128)(2,1)} %basis.1, ...), custom_call_target="tpu_custom_call" | custom-call | flops 2000000000 | bytes 26000000 | tf_op jit(solution)/shard_map/local_stencil/pallas_call | solution.py:199
  26.8 0.0 collective-permute-done.2.before
  26.8 0.0 collective-permute-done.3.after
  26.8 1.3 %edge_gram.2 = (bf16[6,2,32,720]{3,2,1,0:T(8,128)(2,1)S(1)}, f32[32,32]{1,0:T(8,128)S(1)}) custom-call(f32[2,2,2,8,2160]{4,3,2,1,0:T(8,128)S(1)} %collective-permute-done.2.before, f32[2,2,2,8,2160]{4,3,2,1,0:T(8,128)S(1)} %collective-permute-done.3.after, f32[12,2,32,720]{3,2,1,0:T(8,128)S(1)} %get-tuple-element.22.part, ...), custom_call_target="tpu_custom_call" | custom-call | flops 100000000 | bytes 6000000 | tf_op jit(solution)/shard_map/edge_gram/pallas_call | solution.py:283
  28.1 0.6 %collective-permute-done.before = f32[2,2,2,8,2160]{4,3,2,1,0:T(8,128)S(1)} collective-permute-done((f32[2,2,2,8,2160]{4,3,2,1,0:T(8,128)}, f32[2,2,2,8,2160]{4,3,2,1,0:T(8,128)S(1)}, u32[]{:S(2)}, u32[]{:S(2)}) %collective-permute-start) | collective-permute-done | bytes 552992 | tf_op jit(solution)/shard_map/ppermute | solution.py:456
  28.7 0.6 %collective-permute-done.1.after = f32[2,2,2,8,2160]{4,3,2,1,0:T(8,128)S(1)} collective-permute-done((f32[2,2,2,8,2160]{4,3,2,1,0:T(8,128)}, f32[2,2,2,8,2160]{4,3,2,1,0:T(8,128)S(1)}, u32[]{:S(2)}, u32[]{:S(2)}) %collective-permute-start.1) | collective-permute-done | bytes 552992 | tf_op jit(solution)/shard_map/ppermute | solution.py:456
  29.3 1.4 %edge_gram.3 = (bf16[6,2,32,720]{3,2,1,0:T(8,128)(2,1)S(1)}, f32[32,8,128]{2,1,0:T(8,128)S(1)}) custom-call(f32[2,2,2,8,2160]{4,3,2,1,0:T(8,128)S(1)} %collective-permute-done.before, f32[2,2,2,8,2160]{4,3,2,1,0:T(8,128)S(1)} %collective-permute-done.1.after, f32[12,2,32,720]{3,2,1,0:T(8,128)S(1)} %get-tuple-element.22.part, ...), custom_call_target="tpu_custom_call" | custom-call | flops 100000000 | bytes 6000000 | tf_op jit(solution)/shard_map/edge_gram/pallas_call | solution.py:283
  30.7 14.6 %all_to_all.5.grams = f32[32,8,128]{2,1,0:T(8,128)S(1)} all-to-all(f32[32,8,128]{2,1,0:T(8,128)S(1)} %get-tuple-element.26), channel_id=1, replica_groups=mesh['band'=4,'tile'=8] {'band','tile'}, dimensions={0} | all-to-all | bytes 262144 | tf_op jit(solution)/shard_map/all_to_all | solution.py:468
  45.3 8.2 %frame_project.1 = f32[24,12,2,8,720]{4,3,2,1,0:T(8,128)} custom-call(f32[32,8,128]{2,1,0:T(8,128)S(1)} %all_to_all.5.grams, bf16[12,2,96,720]{3,2,1,0:T(8,128)(2,1)S(1)} %get-tuple-element.27.basis_inner, bf16[12,2,96,720]{3,2,1,0:T(8,128)(2,1)S(1)} %get-tuple-element.23.basis_edge, bf16[12,2,32,720]{3,2,1,0:T(8,128)(2,1)S(1)} %get-tuple-element.28.inner, ...), custom_call_target="tpu_custom_call" | custom-call | tf_op jit(solution)/shard_map/frame_project/pallas_call | solution.py:429
  (4 shorter events, 0.0 us)
Async XLA Ops:
  1.6 4.6 %copy-start = (f32[2,2,2,8,2160]{4,3,2,1,0:T(8,128)}, f32[2,2,2,8,2160]{4,3,2,1,0:T(8,128)S(1)}, u32[]{:S(2)}) copy-start(f32[2,2,2,8,2160]{4,3,2,1,0:T(8,128)S(1)} %get-tuple-element.19.refs_1_) | copy-start | bytes 1658884
  1.7 10.7 %copy-start.1 = (s32[8,720]{1,0:T(8,128)S(1)}, s32[8,720]{1,0:T(8,128)}, u32[]{:S(2)}) copy-start(s32[8,720]{1,0:T(8,128)} %param.5) | copy-start | bytes 69124
  1.7 25.1 %collective-permute-start.2 = (f32[2,2,2,8,2160]{4,3,2,1,0:T(8,128)S(1)}, f32[2,2,2,8,2160]{4,3,2,1,0:T(8,128)S(1)}, u32[]{:S(2)}, u32[]{:S(2)}) collective-permute-start(f32[2,2,2,8,2160]{4,3,2,1,0:T(8,128)S(1)} %get-tuple-element.18.refs_0_), channel_id=1, source_target_pairs={{0,1},{1,2},{2,3},{3,4},{4,5},{5,6},{6,7},{7,0},{8,9},{9,10},{10,1... | collective-permute-start | bytes 1658888 | tf_op jit(solution)/shard_map/ppermute | solution.py:456
  2.2 24.6 %collective-permute-start.3 = (f32[2,2,2,8,2160]{4,3,2,1,0:T(8,128)S(1)}, f32[2,2,2,8,2160]{4,3,2,1,0:T(8,128)S(1)}, u32[]{:S(2)}, u32[]{:S(2)}) collective-permute-start(f32[2,2,2,8,2160]{4,3,2,1,0:T(8,128)S(1)} %get-tuple-element.19.refs_1_), channel_id=1, source_target_pairs={{1,0},{2,1},{3,2},{4,3},{5,4},{6,5},{7,6},{0,7},{9,8},{10,9},{11,1... | collective-permute-start | bytes 1658888 | tf_op jit(solution)/shard_map/ppermute | solution.py:456
  8.8 19.9 %collective-permute-start = (f32[2,2,2,8,2160]{4,3,2,1,0:T(8,128)}, f32[2,2,2,8,2160]{4,3,2,1,0:T(8,128)S(1)}, u32[]{:S(2)}, u32[]{:S(2)}) collective-permute-start(f32[2,2,2,8,2160]{4,3,2,1,0:T(8,128)} %get-tuple-element.20), channel_id=1, source_target_pairs={{0,1},{1,2},{2,3},{3,4},{4,5},{5,6},{6,7},{7,0},{8,9},{9,10},{10,1... | collective-permute-start | bytes 1658888 | tf_op jit(solution)/shard_map/ppermute | solution.py:456
  8.9 20.4 %collective-permute-start.1 = (f32[2,2,2,8,2160]{4,3,2,1,0:T(8,128)}, f32[2,2,2,8,2160]{4,3,2,1,0:T(8,128)S(1)}, u32[]{:S(2)}, u32[]{:S(2)}) collective-permute-start(f32[2,2,2,8,2160]{4,3,2,1,0:T(8,128)} %get-tuple-element.21), channel_id=1, source_target_pairs={{1,0},{2,1},{3,2},{4,3},{5,4},{6,5},{7,6},{0,7},{9,8},{10,9},{11,1... | collective-permute-start | bytes 1658888 | tf_op jit(solution)/shard_map/ppermute | solution.py:456

commit v6 on v5

--- a/solution.py
+++ b/solution.py
@@ -41,8 +41,12 @@
     return lat // 128 * 128
 
 
+def odd_tile():
+    return lax.axis_index("tile") % 2
+
+
 def pack_kernel(first, winds, *refs):
-    up, down, held, sems = refs[-4:]
+    far, near, held, sems = refs[-4:]
     fields, snaps = winds.shape[:2]
     turns, turn, lat = held.shape[0], held.shape[4], held.shape[6]
     main = whole_lanes(lat)
@@ -56,7 +60,9 @@
                 )
             )
             pulls[-1].start()
-    odd = rows_of((LON, lat)) % 2 == 1
+    row = rows_of((LON, lat))
+    odd = row % 2 == 1
+    upward = jnp.zeros_like(row) + odd_tile() == 1
     for n in range(turns):
         pulls[2 * n].wait()
         pulls[2 * n + 1].wait()
@@ -64,16 +70,17 @@
             for g in range(snaps // 4):
                 tails = ([], [])
                 for i in range(turn):
-                    low = [held[n, 0, f, 4 * g + t, i] for t in (0, 2, 1, 3)]
+                    low = [held[n, 0, f, 4 * g + t, i] for t in (0, 3, 1, 2)]
                     low = jnp.concatenate(low, axis=0)
                     low = jnp.where(odd, 8.0 * pltpu.roll(low, 1, 0), 0.0) - low
                     high = [held[n, 1, f, 4 * g + t, i] for t in (2, 0, 3, 1)]
                     high = jnp.concatenate(high, axis=0)
                     high = high - jnp.where(odd, 0.0, 8.0 * pltpu.roll(high, 7, 0))
-                    for ref, tail, tile in ((down, tails[0], low), (up, tails[1], high)):
+                    pair = (jnp.where(upward, high, low), jnp.where(upward, low, high))
+                    for ref, tail, tile in zip((far, near), tails, pair):
                         ref[f, n, g, :, i * main : (i + 1) * main] = tile[:, :main]
                         tail.append(tile[:, main:])
-                for ref, tail in ((down, tails[0]), (up, tails[1])):
+                for ref, tail in zip((far, near), tails):
                     ref[f, n, g, :, turn * main :] = jnp.concatenate(tail, axis=1)
 
 
@@ -220,16 +227,16 @@
 
 
 def edge_kernel(
-    first, last, before, after, part, basis_edge, ground, rows, gram, snap, out, acc
+    first, last, far, near, part, basis_edge, ground, rows, gram, snap, out, acc
 ):
     fields, height, lat = part.shape[1:]
-    turns, groups = before.shape[1:3]
+    turns, groups = far.shape[1:3]
     turn = snap.shape[0] // turns
     main = whole_lanes(lat)
     rank = gram.shape[0] - height // HALF
     acc[...] = jnp.zeros_like(acc)
     row = rows_of((LON, lat))
-    from_after = row % HALF < 2
+    from_near = row % HALF // 2 == odd_tile()
 
     def tile(halo, n, f, g, i):
         start = turn * main + i * (lat - main)
@@ -249,11 +256,9 @@
             for f in range(fields):
                 tiles = []
                 for g in range(groups):
-                    high, low = tile(before, n, 1 - f, g, i), tile(after, n, 1 - f, g, i)
-                    tiles.append(jnp.where(from_after, low, high))
-                    tiles.append(
-                        jnp.where(from_after, pltpu.roll(low, 6, 0), pltpu.roll(high, 2, 0))
-                    )
+                    one, two = tile(far, n, 1 - f, g, i), tile(near, n, 1 - f, g, i)
+                    tiles.append(jnp.where(from_near, two, one))
+                    tiles.append(pltpu.roll(jnp.where(from_near, one, two), 2, 0))
                 tiles = [
                     part[level, f, LON * p : LON * (p + 1)] + x * scale
                     for p, x in enumerate(tiles)
@@ -274,7 +279,7 @@
     out[...] = jnp.broadcast_to(lined[None], out.shape)
 
 
-def edges(before, after, part, basis_edge, ground, rows, gram, first, count, devices):
+def edges(far, near, part, basis_edge, ground, rows, gram, first, count, devices):
     levels, fields, height, lat = part.shape
     cols = gram.shape[0]
     last = first + count == levels
@@ -294,7 +299,7 @@
             flops=10**8, bytes_accessed=6 * 10**6, transcendentals=0
         ),
         name="edge_gram",
-    )(before, after, part, basis_edge, ground, rows, gram)
+    )(far, near, part, basis_edge, ground, rows, gram)
 
 
 def spread_lane(block, j):
@@ -446,14 +451,14 @@
     levels, lat = winds.shape[2], winds.shape[4]
     tiles = lax.axis_size("tile")
     devices = tiles * lax.axis_size("band")
-    up_pairs = [(i, (i + 1) % tiles) for i in range(tiles)]
-    down_pairs = [(j, i) for i, j in up_pairs]
+    far_pairs = [(i, (i + 1 if i % 2 else i - 1) % tiles) for i in range(tiles)]
+    near_pairs = [(i, i ^ 1) for i in range(tiles)]
 
     spans = spans_of(levels)
     halos, packed = [], ()
     for first, count in spans:
-        up, down = packed = pack(winds, first, count, packed)
-        halos.append((lax.ppermute(up, "tile", up_pairs), lax.ppermute(down, "tile", down_pairs)))
+        far, near = packed = pack(winds, first, count, packed)
+        halos.append((lax.ppermute(far, "tile", far_pairs), lax.ppermute(near, "tile", near_pairs)))
 
     cosine = jnp.cos((jnp.arange(lat, dtype=F32) + 0.5) * (jnp.pi / lat) - jnp.pi / 2)
     rows = jnp.stack([cosine, jnp.sqrt(cosine) / cosine / 12.0])

time: 53.9 us -> 53.8 us (level)
  waiting for transfers between devices: 1.17 us -> 5.16 us
  starting transfers between devices: 8.2 us -> 5.37 us
  blocking collectives: 14.6 us -> 13.4 us
    ppermute x4, waiting for transfers between devices: 1.17 us -> 5.16 us  [the longest x2 5.15 us: on_device(): lax.ppermute(far, 'tile', far_pairs)]
    ppermute x4, starting transfers between devices: 8.2 us -> 5.37 us  [the longest x2 5.37 us: on_device(): lax.ppermute(far, 'tile', far_pairs)]
    all_to_all x1, blocking collectives: 14.6 us -> 13.4 us  [on_device(): grams = lax.all_to_all(gram, ('band', 'tile'), 0, 0)]
  transfers between devices with their start and end apart: 4 -> 4, of which waited for: 2 -> 1; matrix products, arithmetic and copies ran while one was open for 1% -> 1% of each run, Pallas kernels for 33% -> 34%
where the time goes in v6:
time: 53.8 us; the launch traced here: 53.4 us
  Pallas kernels  29.1 us (54%)
  blocking collectives  13.4 us (25%)
  starting transfers between devices  5.37 us (10%)
  waiting for transfers between devices  5.16 us (10%)
    pallas_call x1, Pallas kernels, local(): pl.pallas_call(local_kernel, grid=(levels,), in_specs=[pl.BlockSpec((fiel...  14.1 us
    all_to_all x1, blocking collectives, on_device(): grams = lax.all_to_all(gram, ('band', 'tile'), 0, 0)  13.4 us
    pallas_call x1, Pallas kernels, final(): pl.pallas_call(final_kernel, in_specs=[pl.BlockSpec(memory_space=pltpu.VM...  8.2 us
    ppermute x2, starting transfers between devices, on_device(): lax.ppermute(far, 'tile', far_pairs)  5.37 us
    ppermute x2, waiting for transfers between devices, on_device(): lax.ppermute(far, 'tile', far_pairs)  5.15 us
    pallas_call x2, Pallas kernels, pack(): pl.pallas_call(functools.partial(pack_kernel, first), in_specs=[pl.BlockS...  4.17 us
    pallas_call x2, Pallas kernels, edges(): pl.pallas_call(functools.partial(edge_kernel, first, last), in_specs=[who...  2.68 us
  transfers between devices with their start and end apart: 4, of which 1 were waited for; matrix products, arithmetic and copies ran while one was open for 1% of the time, Pallas kernels for 34%

profile of v6, /device:TPU:0, one launch (start us, length us, event | category | flops | bytes accessed | tf_op | source)
XLA Modules:
  0.0 53.4 jit_solution(13247904790594744571)
XLA Ops:
  0.0 1.6 %pack_halo.2 = (f32[2,2,2,8,2160]{4,3,2,1,0:T(8,128)S(1)}, f32[2,2,2,8,2160]{4,3,2,1,0:T(8,128)S(1)}) custom-call(f32[2,8,12,8,720]{4,3,2,1,0:T(8,128)} %winds.5), custom_call_target="tpu_custom_call" | custom-call | tf_op jit(solution)/shard_map/pack_halo/pallas_call | solution.py:93
  1.6 0.0 copy-start
  1.6 0.0 copy-start.1
  1.6 4.6 %collective-permute-start.2 = (f32[2,2,2,8,2160]{4,3,2,1,0:T(8,128)S(1)}, f32[2,2,2,8,2160]{4,3,2,1,0:T(8,128)S(1)}, u32[]{:S(2)}, u32[]{:S(2)}) collective-permute-start(f32[2,2,2,8,2160]{4,3,2,1,0:T(8,128)S(1)} %get-tuple-element.18.refs_0_), channel_id=1, source_target_pairs={{0,7},{1,2},{2,1},{3,4},{4,3},{5,6},{6,5},{7,0},{8,15},{9,10},{10,... | collective-permute-start | bytes 1658888 | tf_op jit(solution)/shard_map/ppermute | solution.py:461
  6.2 0.0 collective-permute-start.3
  6.2 0.0 copy-done
  6.2 2.6 %pack_halo.3 = (f32[2,2,2,8,2160]{4,3,2,1,0:T(8,128)}, f32[2,2,2,8,2160]{4,3,2,1,0:T(8,128)}) custom-call(f32[2,8,12,8,720]{4,3,2,1,0:T(8,128)} %winds.5, f32[2,2,2,8,2160]{4,3,2,1,0:T(8,128)S(1)} %get-tuple-element.18.refs_0_, f32[2,2,2,8,2160]{4,3,2,1,0:T(8,128)} %copy-done), custom_call_target="tpu_custom_call" | custom-call | tf_op jit(solution)/shard_map/pack_halo/pallas_call | solution.py:93
  8.8 0.8 %collective-permute-start = (f32[2,2,2,8,2160]{4,3,2,1,0:T(8,128)}, f32[2,2,2,8,2160]{4,3,2,1,0:T(8,128)S(1)}, u32[]{:S(2)}, u32[]{:S(2)}) collective-permute-start(f32[2,2,2,8,2160]{4,3,2,1,0:T(8,128)} %get-tuple-element.20), channel_id=1, source_target_pairs={{0,7},{1,2},{2,1},{3,4},{4,3},{5,6},{6,5},{7,0},{8,15},{9,10},{10,... | collective-permute-start | bytes 1658888 | tf_op jit(solution)/shard_map/ppermute | solution.py:461
  9.6 0.0 collective-permute-start.1
  9.6 0.0 copy-done.1
  9.6 0.1 fusion
  9.7 0.1 pad.6.clone
  9.8 0.1 maximum_maximum_fusion.rows
  9.9 14.1 %local_stencil.1 = (f32[12,2,32,720]{3,2,1,0:T(8,128)S(1)}, bf16[12,2,96,720]{3,2,1,0:T(8,128)(2,1)S(1)}, bf16[12,2,32,720]{3,2,1,0:T(8,128)(2,1)S(1)}, bf16[12,2,96,720]{3,2,1,0:T(8,128)(2,1)S(1)}, f32[32,32]{1,0:T(8,128)S(1)}) custom-call(f32[2,8,12,8,720]{4,3,2,1,0:T(8,128)} %winds.5, bf16[24,12,2,8,720]{4,3,2,1,0:T(8,128)(2,1)} %basis.1, ...), custom_call_target="tpu_custom_call" | custom-call | flops 2000000000 | bytes 26000000 | tf_op jit(solution)/shard_map/local_stencil/pallas_call | solution.py:206
  24.0 0.0 collective-permute-done.2.far
  24.0 0.0 collective-permute-done.3.near
  24.0 1.3 %edge_gram.2 = (bf16[6,2,32,720]{3,2,1,0:T(8,128)(2,1)S(1)}, f32[32,32]{1,0:T(8,128)S(1)}) custom-call(f32[2,2,2,8,2160]{4,3,2,1,0:T(8,128)S(1)} %collective-permute-done.2.far, f32[2,2,2,8,2160]{4,3,2,1,0:T(8,128)S(1)} %collective-permute-done.3.near, f32[12,2,32,720]{3,2,1,0:T(8,128)S(1)} %get-tuple-element.22.part, ...), custom_call_target="tpu_custom_call" | custom-call | flops 100000000 | bytes 6000000 | tf_op jit(solution)/shard_map/edge_gram/pallas_call | solution.py:288
  25.3 5.2 %collective-permute-done.far = f32[2,2,2,8,2160]{4,3,2,1,0:T(8,128)S(1)} collective-permute-done((f32[2,2,2,8,2160]{4,3,2,1,0:T(8,128)}, f32[2,2,2,8,2160]{4,3,2,1,0:T(8,128)S(1)}, u32[]{:S(2)}, u32[]{:S(2)}) %collective-permute-start) | collective-permute-done | bytes 552992 | tf_op jit(solution)/shard_map/ppermute | solution.py:461
  30.5 0.0 collective-permute-done.1.near
  30.5 1.4 %edge_gram.3 = (bf16[6,2,32,720]{3,2,1,0:T(8,128)(2,1)S(1)}, f32[32,8,128]{2,1,0:T(8,128)S(1)}) custom-call(f32[2,2,2,8,2160]{4,3,2,1,0:T(8,128)S(1)} %collective-permute-done.far, f32[2,2,2,8,2160]{4,3,2,1,0:T(8,128)S(1)} %collective-permute-done.1.near, f32[12,2,32,720]{3,2,1,0:T(8,128)S(1)} %get-tuple-element.22.part, ...), custom_call_target="tpu_custom_call" | custom-call | flops 100000000 | bytes 6000000 | tf_op jit(solution)/shard_map/edge_gram/pallas_call | solution.py:288
  31.9 13.4 %all_to_all.5.grams = f32[32,8,128]{2,1,0:T(8,128)S(1)} all-to-all(f32[32,8,128]{2,1,0:T(8,128)S(1)} %get-tuple-element.26), channel_id=1, replica_groups=mesh['band'=4,'tile'=8] {'band','tile'}, dimensions={0} | all-to-all | bytes 262144 | tf_op jit(solution)/shard_map/all_to_all | solution.py:473
  45.2 8.2 %frame_project.1 = f32[24,12,2,8,720]{4,3,2,1,0:T(8,128)} custom-call(f32[32,8,128]{2,1,0:T(8,128)S(1)} %all_to_all.5.grams, bf16[12,2,96,720]{3,2,1,0:T(8,128)(2,1)S(1)} %get-tuple-element.27.basis_inner, bf16[12,2,96,720]{3,2,1,0:T(8,128)(2,1)S(1)} %get-tuple-element.23.basis_edge, bf16[12,2,32,720]{3,2,1,0:T(8,128)(2,1)S(1)} %get-tuple-element.28.inner, ...), custom_call_target="tpu_custom_call" | custom-call | tf_op jit(solution)/shard_map/frame_project/pallas_call | solution.py:434
  (4 shorter events, 0.0 us)
Async XLA Ops:
  1.6 4.6 %copy-start = (f32[2,2,2,8,2160]{4,3,2,1,0:T(8,128)}, f32[2,2,2,8,2160]{4,3,2,1,0:T(8,128)S(1)}, u32[]{:S(2)}) copy-start(f32[2,2,2,8,2160]{4,3,2,1,0:T(8,128)S(1)} %get-tuple-element.19.refs_1_) | copy-start | bytes 1658884
  1.6 8.0 %copy-start.1 = (s32[8,720]{1,0:T(8,128)S(1)}, s32[8,720]{1,0:T(8,128)}, u32[]{:S(2)}) copy-start(s32[8,720]{1,0:T(8,128)} %param.5) | copy-start | bytes 69124
  1.6 22.4 %collective-permute-start.2 = (f32[2,2,2,8,2160]{4,3,2,1,0:T(8,128)S(1)}, f32[2,2,2,8,2160]{4,3,2,1,0:T(8,128)S(1)}, u32[]{:S(2)}, u32[]{:S(2)}) collective-permute-start(f32[2,2,2,8,2160]{4,3,2,1,0:T(8,128)S(1)} %get-tuple-element.18.refs_0_), channel_id=1, source_target_pairs={{0,7},{1,2},{2,1},{3,4},{4,3},{5,6},{6,5},{7,0},{8,15},{9,10},{10,... | collective-permute-start | bytes 1658888 | tf_op jit(solution)/shard_map/ppermute | solution.py:461
  6.2 17.8 %collective-permute-start.3 = (f32[2,2,2,8,2160]{4,3,2,1,0:T(8,128)S(1)}, f32[2,2,2,8,2160]{4,3,2,1,0:T(8,128)S(1)}, u32[]{:S(2)}, u32[]{:S(2)}) collective-permute-start(f32[2,2,2,8,2160]{4,3,2,1,0:T(8,128)S(1)} %get-tuple-element.19.refs_1_), channel_id=1, source_target_pairs={{0,1},{1,0},{2,3},{3,2},{4,5},{5,4},{6,7},{7,6},{8,9},{9,8},{10,11... | collective-permute-start | bytes 1658888 | tf_op jit(solution)/shard_map/ppermute | solution.py:461
  8.8 21.7 %collective-permute-start = (f32[2,2,2,8,2160]{4,3,2,1,0:T(8,128)}, f32[2,2,2,8,2160]{4,3,2,1,0:T(8,128)S(1)}, u32[]{:S(2)}, u32[]{:S(2)}) collective-permute-start(f32[2,2,2,8,2160]{4,3,2,1,0:T(8,128)} %get-tuple-element.20), channel_id=1, source_target_pairs={{0,7},{1,2},{2,1},{3,4},{4,3},{5,6},{6,5},{7,0},{8,15},{9,10},{10,... | collective-permute-start | bytes 1658888 | tf_op jit(solution)/shard_map/ppermute | solution.py:461
  9.6 20.9 %collective-permute-start.1 = (f32[2,2,2,8,2160]{4,3,2,1,0:T(8,128)}, f32[2,2,2,8,2160]{4,3,2,1,0:T(8,128)S(1)}, u32[]{:S(2)}, u32[]{:S(2)}) collective-permute-start(f32[2,2,2,8,2160]{4,3,2,1,0:T(8,128)} %get-tuple-element.21), channel_id=1, source_target_pairs={{0,1},{1,0},{2,3},{3,2},{4,5},{5,4},{6,7},{7,6},{8,9},{9,8},{10,11... | collective-permute-start | bytes 1658888 | tf_op jit(solution)/shard_map/ppermute | solution.py:461
